TPU v7x, 32 devices: a whole 2x2x4 slice. The times are simulated.
32 devices in a mesh: dp: 4 (over y, x), expert: 8 (over z, core).
Axes of the slice: x: 2, y: 2, z: 4, core: 2. Of those that a mesh axis runs over, the one named last changes fastest.
Arguments:
- tokens: bfloat16 [4096, 2048], P(('dp', 'expert')), may hold values from -6 to 6
- routes: int32 [4096, 8], P(('dp', 'expert')), may hold values from 0 to 15, all different within a row; in each aligned block of 128 rows (0 to 127, 128 to 255, ...) at most 65 rows name the same one
- route_gates: float32 [4096, 8], P(('dp', 'expert')), may hold values from 0.05 to 0.45
- gate_matrix: bfloat16 [16, 2048, 768], P('expert'), may hold values from -0.125 to 0.125
- up_matrix: bfloat16 [16, 2048, 768], P('expert'), may hold values from -0.125 to 0.125
- down_matrix: bfloat16 [16, 768, 2048], P('expert'), may hold values from -0.21875 to 0.21875
- cotangent: bfloat16 [4096, 2048], P(('dp', 'expert')), may hold values from -6 to 6
Outputs:
- layer_out: bfloat16 [4096, 2048], P(('dp', 'expert'))
- grad_tokens: bfloat16 [4096, 2048], P(('dp', 'expert'))
- grad_gate: bfloat16 [16, 2048, 768], P('expert', 'dp')
- grad_up: bfloat16 [16, 2048, 768], P('expert', 'dp')
- grad_down: bfloat16 [16, 768, 2048], P('expert', None, 'dp')
Inputs may be any that keep to these rules, and one draw needn't show every extreme that they name: `routes`: each row names 8 different experts. Among the 128 rows of one device no expert is named more than 65 times, and in every draw some expert is named exactly 65 times by the rows of some device.
All inputs are finite; a program needn't handle non-finite values.
Results may differ from a plain program's by a relative error of at most 0.013.
Values may be sent and summed in bfloat16 or wider, within the bound.
A program may use at most 256 MiB of HBM per device.

v0:
```python
import jax
import jax.numpy as jnp
from jax import lax
from jax.sharding import PartitionSpec as P


def expert_pass(rows_in, scaled, gate_matrix, up_matrix, down_matrix):
    pre_gate = jnp.einsum("erd,edf->erf", rows_in, gate_matrix, preferred_element_type=jnp.float32)
    pre_up = jnp.einsum("erd,edf->erf", rows_in, up_matrix, preferred_element_type=jnp.float32)
    sigmoid_gate = jax.nn.sigmoid(pre_gate)
    activated = pre_gate * sigmoid_gate
    hidden = (activated * pre_up).astype(jnp.bfloat16)
    produced = jnp.einsum(
        "erf,efd->erd", hidden, down_matrix, preferred_element_type=jnp.float32
    ).astype(jnp.bfloat16)
    grad_hidden = jnp.einsum(
        "erd,efd->erf", scaled, down_matrix, preferred_element_type=jnp.float32
    )
    grad_pregate = (
        grad_hidden * pre_up * sigmoid_gate * (1.0 + pre_gate * (1.0 - sigmoid_gate))
    ).astype(jnp.bfloat16)
    grad_preup = (grad_hidden * activated).astype(jnp.bfloat16)
    returned = (
        jnp.einsum("erf,edf->erd", grad_pregate, gate_matrix, preferred_element_type=jnp.float32)
        + jnp.einsum("erf,edf->erd", grad_preup, up_matrix, preferred_element_type=jnp.float32)
    ).astype(jnp.bfloat16)
    grad_both = jnp.concatenate([grad_pregate, grad_preup], axis=2)
    return (produced, returned, hidden, grad_both)


def per_device(tokens, routes, route_gates, gate_matrix, up_matrix, down_matrix, cotangent):
    expert_ways = lax.axis_size("expert")
    tok_rows, per_token = routes.shape
    exp_home, width, hidden_units = gate_matrix.shape
    experts_all = exp_home * expert_ways
    capacity = tok_rows * per_token // experts_all + 1
    span_rows = expert_ways * capacity
    slot_count = exp_home * span_rows
    assigned = tok_rows * per_token
    flat_ids = routes.reshape(-1)
    onehot = (flat_ids[:, None] == jnp.arange(experts_all, dtype=jnp.int32)[None, :]).astype(
        jnp.int32
    )
    earlier = jnp.cumsum(onehot, axis=0) - onehot
    position_in = jnp.sum(earlier * onehot, axis=1)
    slot_of = flat_ids % exp_home * span_rows + flat_ids // exp_home * capacity + position_in
    source = (
        jnp.zeros((slot_count,), jnp.int32)
        .at[slot_of]
        .set(jnp.arange(assigned, dtype=jnp.int32) + 1)
    )
    filled = source > 0
    assign_of = jnp.maximum(source - 1, 0)
    token_of = assign_of // per_token
    gate_of = jnp.where(filled, route_gates.reshape(-1)[assign_of], 0.0)
    send_rows = jnp.where(filled[:, None], tokens[token_of], jnp.zeros((), jnp.bfloat16)).reshape(
        exp_home, span_rows, width
    )
    send_scaled = (
        (gate_of[:, None] * cotangent[token_of].astype(jnp.float32))
        .astype(jnp.bfloat16)
        .reshape(exp_home, span_rows, width)
    )
    rows_in, scaled = (
        lax.all_to_all(send_rows, "expert", split_axis=1, concat_axis=1, tiled=True),
        lax.all_to_all(send_scaled, "expert", split_axis=1, concat_axis=1, tiled=True),
    )
    produced, returned, hidden, grad_both = expert_pass(
        rows_in, scaled, gate_matrix, up_matrix, down_matrix
    )
    got_out, got_back = (
        lax.all_to_all(produced, "expert", split_axis=1, concat_axis=1, tiled=True),
        lax.all_to_all(returned, "expert", split_axis=1, concat_axis=1, tiled=True),
    )
    out_rows = got_out.reshape(slot_count, width)[slot_of].reshape(tok_rows, per_token, width)
    layer_out = jnp.sum(route_gates[:, :, None] * out_rows.astype(jnp.float32), axis=1).astype(
        jnp.bfloat16
    )
    back_rows = got_back.reshape(slot_count, width)[slot_of].reshape(tok_rows, per_token, width)
    grad_tokens = jnp.sum(back_rows.astype(jnp.float32), axis=1).astype(jnp.bfloat16)
    whole_both = jnp.einsum("erd,erf->edf", rows_in, grad_both, preferred_element_type=jnp.float32)
    whole_down = jnp.einsum("erd,erf->edf", scaled, hidden, preferred_element_type=jnp.float32)
    summed_both, summed_down = (
        lax.psum_scatter(
            whole_both.astype(jnp.bfloat16), "dp", scatter_dimension=1, tiled=True
        ).astype(jnp.float32),
        lax.psum_scatter(
            whole_down.astype(jnp.bfloat16), "dp", scatter_dimension=1, tiled=True
        ).astype(jnp.float32),
    )
    grad_gate = summed_both[:, :, :hidden_units].astype(jnp.bfloat16)
    grad_up = summed_both[:, :, hidden_units:].astype(jnp.bfloat16)
    grad_down = jnp.transpose(summed_down, (0, 2, 1)).astype(jnp.bfloat16)
    return (layer_out, grad_tokens, grad_gate, grad_up, grad_down)


def solution(mesh):
    in_specs = (
        P(("dp", "expert"), None),
        P(("dp", "expert"), None),
        P(("dp", "expert"), None),
        P("expert", None, None),
        P("expert", None, None),
        P("expert", None, None),
        P(("dp", "expert"), None),
    )
    out_specs = (
        P(("dp", "expert"), None),
        P(("dp", "expert"), None),
        P("expert", "dp", None),
        P("expert", "dp", None),
        P("expert", None, "dp"),
    )
    return jax.shard_map(
        per_device, mesh=mesh, in_specs=in_specs, out_specs=out_specs, check_vma=False
    )
```

profile of v0, /device:TPU:0, one launch (start us, length us, event | category | flops | bytes accessed | tf_op | source)
XLA Modules:
  0.0 555.8 jit_solution(11123925165175378654)
XLA Ops:
  7.2 0.8 copy.65
  8.0 0.1 eq.31
  8.1 0.1 eq.27
  8.2 0.1 reshape.184
  8.3 0.8 copy.64
  9.1 0.1 reshape.187
  9.2 4.5 reduce-window.6
  13.7 0.1 slice.28
  13.8 0.1 copy.68
  14.1 0.1 broadcast_add_fusion
  14.2 4.3 scatter_custom_fusion
  18.6 4.4 gather_fusion.2
  23.0 0.1 broadcast_in_dim.32
  23.1 0.2 copy.70
  23.3 5.7 %gather_fusion = bf16[1040,2048]{1,0:T(8,128)(2,1)} fusion(bf16[128,2048]{1,0:T(8,128)(2,1)S(1)} %copy-done, s32[2048]{0:T(1024)S(1)} %get-tuple-element.40), kind=kCustom, calls=%fused_computation | custom fusion | bytes 8523840 | tf_op jit(solution)/shard_map/gather | solution.py:56
  29.0 18.8 %broadcast_select_fusion = bf16[2,520,2048]{2,0,1:T(2,128)(2,1)} fusion(pred[2,520]{0,1:T(8,128)(4,1)S(1)} %copy.70, bf16[2,520,2048]{2,1,0:T(8,128)(2,1)} %bitcast.45), kind=kLoop, calls=%fused_computation.10 | loop fusion | flops 2129920 | bytes 8520720 | tf_op jit(solution)/shard_map/jit(_where)/select_n | solution.py:56
  47.9 6.7 %all-to-all-start = ((bf16[2,520,2048]{2,0,1:T(2,128)(2,1)}), bf16[2,520,2048]{2,0,1:T(2,128)(2,1)}, u32[]{:S(2)}, u32[]{:S(2)}) async-start(bf16[2,520,2048]{2,0,1:T(2,128)(2,1)} %broadcast_select_fusion), calls=%async_computation | async-start | bytes 8519680 | tf_op jit(solution)/shard_map/all_to_all | solution.py:65
  54.5 0.1 mul.78
  54.6 5.7 %gather_fusion.3 = bf16[1040,2048]{1,0:T(8,128)(2,1)} fusion(bf16[128,2048]{1,0:T(8,128)(2,1)S(1)} %copy-done.2, s32[2048]{0:T(1024)S(1)} %get-tuple-element.40), kind=kCustom, calls=%fused_computation.3 | custom fusion | bytes 8523840 | tf_op jit(solution)/shard_map/gather | solution.py:60
  60.4 3.0 fusion
  63.3 6.4 %copy.77 = bf16[2,520,2048]{2,0,1:T(2,128)(2,1)} copy(bf16[2,520,2048]{2,1,0:T(8,128)(2,1)S(1)} %fusion) | data formatting | bytes 8519680 | tf_op jit(solution)/shard_map/convert_element_type | solution.py:61
  69.7 80.3 %all-to-all-done = bf16[2,520,2048]{2,0,1:T(2,128)(2,1)} async-done(((bf16[2,520,2048]{2,0,1:T(2,128)(2,1)}), bf16[2,520,2048]{2,0,1:T(2,128)(2,1)}, u32[]{:S(2)}, u32[]{:S(2)}) %all-to-all-start) | async-done | bytes 4259872 | tf_op jit(solution)/shard_map/all_to_all | solution.py:65
  150.0 4.6 all-to-all-start.2
  154.6 0.3 reduce-scatter.5.cloned.1.call-start
  154.8 9.8 %fusion.6 = f32[2,520,768]{2,1,0:T(8,128)} fusion(bf16[2,2048,768]{2,1,0:T(8,128)(2,1)} %param.11, bf16[2,520,2048]{2,0,1:T(2,128)(2,1)} %all-to-all-done), kind=kOutput, calls=%fused_computation.20 | convolution fusion | flops 3271557120 | bytes 13746176 | tf_op jit(solution)/shard_map/erd,edf->erf/dot_general | solution.py:9
  164.7 9.9 %fusion.8 = f32[2,520,768]{2,1,0:T(8,128)} fusion(bf16[2,2048,768]{2,1,0:T(8,128)(2,1)} %param.10, bf16[2,520,2048]{2,0,1:T(2,128)(2,1)} %all-to-all-done), kind=kOutput, calls=%fused_computation.22 | convolution fusion | flops 3271557120 | bytes 13746176 | tf_op jit(solution)/shard_map/erd,edf->erf/dot_general | solution.py:8
  174.6 75.4 %all-to-all-done.2 = bf16[2,520,2048]{2,0,1:T(2,128)(2,1)} async-done(((bf16[2,520,2048]{2,0,1:T(2,128)(2,1)}), bf16[2,520,2048]{2,0,1:T(2,128)(2,1)}, u32[]{:S(2)}, u32[]{:S(2)}) %all-to-all-start.2) | async-done | bytes 4259872 | tf_op jit(solution)/shard_map/all_to_all | solution.py:66
  250.0 13.0 %multiply_convert_fusion = (bf16[2,520,768]{2,1,0:T(8,128)(2,1)S(1)}, bf16[2,520,768]{2,1,0:T(8,128)(2,1)}, bf16[2,520,768]{2,1,0:T(8,128)(2,1)S(1)}) fusion(f32[2,520,768]{2,1,0:T(8,128)} %fusion.8, f32[2,520,768]{2,1,0:T(8,128)} %fusion.6, bf16[2,768,2048]{2,1,0:T(8,128)(2,1)} %param.12, bf16[2,520,2048]{2,0,1:T(2,128)(2,1)} %all-to-all-done.2), kind=kOutput, calls=%fused_computation.27 | convolution fusion | flops 3283537920 | bytes 21733376 | tf_op jit(solution)/shard_map/erd,efd->erf/dot_general | solution.py:16
  263.0 1.1 copy-done.9
  264.1 18.6 %convolution_convert_fusion.1 = bf16[2,2048,768]{2,1,0:T(8,128)(2,1)} fusion(bf16[2,520,768]{2,1,0:T(8,128)(2,1)S(1)} %get-tuple-element.34, bf16[2,520,2048]{2,0,1:T(2,128)(2,1)} %all-to-all-done.2), kind=kOutput, calls=%fused_computation.13 | convolution fusion | flops 3274702848 | bytes 12148736 | tf_op jit(solution)/shard_map/erd,erf->edf/dot_general | solution.py:82
  282.8 16.2 %convolution_convert_fusion = bf16[2,2048,1536]{2,1,0:T(8,128)(2,1)} fusion(bf16[2,520,2048]{2,0,1:T(2,128)(2,1)} %all-to-all-done, bf16[2,520,768]{2,1,0:T(8,128)(2,1)S(1)} %get-tuple-element.32, bf16[2,520,768]{2,1,0:T(8,128)(2,1)} %get-tuple-element.33), kind=kOutput, calls=%fused_computation.6 | convolution fusion | flops 6555795456 | bytes 20037632 | tf_op jit(solution)/shard_map/erd,erf->edf/dot_general | solution.py:81
  299.1 7.2 %convolution_convert_fusion.2 = bf16[2,520,2048]{2,1,0:T(8,128)(2,1)S(1)} fusion(bf16[2,520,768]{2,1,0:T(8,128)(2,1)} %copy-done.9, bf16[2,768,2048]{2,1,0:T(8,128)(2,1)} %param.12), kind=kOutput, calls=%fused_computation.15 | convolution fusion | flops 3273687040 | bytes 12148736 | tf_op jit(solution)/shard_map/erf,efd->erd/dot_general | solution.py:13
  306.2 6.3 %copy.74 = bf16[2,520,2048]{2,0,1:T(2,128)(2,1)} copy(bf16[2,520,2048]{2,1,0:T(8,128)(2,1)S(1)} %convolution_convert_fusion.2) | data formatting | bytes 8519680 | tf_op jit(solution)/shard_map/convert_element_type | solution.py:15
  312.6 4.9 all-to-all-start.1
  317.5 8.7 %fusion.26 = f32[2,520,2048]{2,1,0:T(8,128)} fusion(bf16[2,520,768]{2,1,0:T(8,128)(2,1)S(1)} %copy-done.8, bf16[2,2048,768]{2,1,0:T(8,128)(2,1)} %param.10), kind=kOutput, calls=%fused_computation.65 | convolution fusion | flops 3271557120 | bytes 16408576 | tf_op jit(solution)/shard_map/erf,edf->erd/dot_general | solution.py:24
  326.2 7.9 %add_convert_fusion = bf16[2,520,2048]{2,1,0:T(8,128)(2,1)S(1)} fusion(f32[2,520,2048]{2,1,0:T(8,128)} %fusion.26, bf16[2,520,768]{2,1,0:T(8,128)(2,1)S(1)} %copy-done.7, bf16[2,2048,768]{2,1,0:T(8,128)(2,1)} %param.11), kind=kOutput, calls=%fused_computation.9 | convolution fusion | flops 3275816960 | bytes 20668416 | tf_op jit(solution)/shard_map/erf,edf->erd/dot_general | solution.py:25
  334.1 6.3 %copy.79 = bf16[2,520,2048]{2,0,1:T(2,128)(2,1)} copy(bf16[2,520,2048]{2,1,0:T(8,128)(2,1)S(1)} %add_convert_fusion) | data formatting | bytes 8519680 | tf_op jit(solution)/shard_map/convert_element_type | solution.py:26
  340.4 72.4 %all-to-all-done.1 = bf16[2,520,2048]{2,0,1:T(2,128)(2,1)} async-done(((bf16[2,520,2048]{2,0,1:T(2,128)(2,1)}), bf16[2,520,2048]{2,0,1:T(2,128)(2,1)}, u32[]{:S(2)}, u32[]{:S(2)}) %all-to-all-start.1) | async-done | bytes 4259872 | tf_op jit(solution)/shard_map/all_to_all | solution.py:72
  412.9 4.8 all-to-all-start.3
  417.7 6.1 %copy.75 = bf16[2,520,2048]{2,1,0:T(8,128)(2,1)} copy(bf16[2,520,2048]{2,0,1:T(2,128)(2,1)} %all-to-all-done.1) | data formatting | bytes 8519680 | tf_op jit(solution)/shard_map/all_to_all | solution.py:72
  423.8 11.7 %gather_fusion.1 = bf16[1024,2048]{1,0:T(8,128)(2,1)} fusion(bf16[1040,2048]{1,0:T(8,128)(2,1)} %bitcast.43, s32[1024]{0:T(1024)S(1)} %broadcast_clamp_fusion), kind=kCustom, calls=%fused_computation.1 | custom fusion | bytes 8392704 | tf_op jit(solution)/shard_map/gather | solution.py:75
  435.5 77.7 %all-to-all-done.3 = bf16[2,520,2048]{2,0,1:T(2,128)(2,1)} async-done(((bf16[2,520,2048]{2,0,1:T(2,128)(2,1)}), bf16[2,520,2048]{2,0,1:T(2,128)(2,1)}, u32[]{:S(2)}, u32[]{:S(2)}) %all-to-all-start.3) | async-done | bytes 4259872 | tf_op jit(solution)/shard_map/all_to_all | solution.py:73
  513.1 6.1 %copy.80 = bf16[2,520,2048]{2,1,0:T(8,128)(2,1)} copy(bf16[2,520,2048]{2,0,1:T(2,128)(2,1)} %all-to-all-done.3) | data formatting | bytes 8519680 | tf_op jit(solution)/shard_map/all_to_all | solution.py:73
  519.2 11.9 %gather_fusion.4 = bf16[1024,2048]{1,0:T(8,128)(2,1)} fusion(bf16[1040,2048]{1,0:T(8,128)(2,1)} %bitcast.42, s32[1024]{0:T(1024)S(1)} %broadcast_clamp_fusion), kind=kCustom, calls=%fused_computation.4 | custom fusion | bytes 8392704 | tf_op jit(solution)/shard_map/gather | solution.py:79
  531.1 6.0 %bitcast_reduce_fusion = bf16[128,2048]{1,0:T(8,128)(2,1)} fusion(bf16[1024,2048]{1,0:T(8,128)(2,1)} %gather_fusion.4), kind=kLoop, calls=%fused_computation.14 | loop fusion | flops 1835008 | bytes 4718592 | tf_op jit(solution)/shard_map/reduce_sum | solution.py:80
  537.1 5.2 fusion.1
  542.3 2.6 copy.83
  544.9 3.7 fusion.25
  (35 shorter events, 0.3 us)
Async XLA Ops:
  7.2 16.1 %copy-start = (bf16[128,2048]{1,0:T(8,128)(2,1)S(1)}, bf16[128,2048]{1,0:T(8,128)(2,1)}, u32[]{:S(2)}) copy-start(bf16[128,2048]{1,0:T(8,128)(2,1)} %param.7) | copy-start | bytes 1572868
  9.1 13.8 %copy-start.4 = (f32[128,8]{1,0:T(8,128)}, f32[128,8]{1,0:T(8,128)S(1)}, u32[]{:S(2)}) copy-start(f32[128,8]{1,0:T(8,128)S(1)} %copy.64) | copy-start | bytes 12292
  47.9 6.8 %copy-start.2 = (bf16[128,2048]{1,0:T(8,128)(2,1)S(1)}, bf16[128,2048]{1,0:T(8,128)(2,1)}, u32[]{:S(2)}) copy-start(bf16[128,2048]{1,0:T(8,128)(2,1)} %param.13) | copy-start | bytes 1572868
  47.9 102.1 %all-to-all-start = ((bf16[2,520,2048]{2,0,1:T(2,128)(2,1)}), bf16[2,520,2048]{2,0,1:T(2,128)(2,1)}, u32[]{:S(2)}, u32[]{:S(2)}) async-start(bf16[2,520,2048]{2,0,1:T(2,128)(2,1)} %broadcast_select_fusion), calls=%async_computation | async-start | bytes 8519680 | tf_op jit(solution)/shard_map/all_to_all | solution.py:65
  150.0 100.0 %all-to-all-start.2 = ((bf16[2,520,2048]{2,0,1:T(2,128)(2,1)}), bf16[2,520,2048]{2,0,1:T(2,128)(2,1)}, u32[]{:S(2)}, u32[]{:S(2)}) async-start(bf16[2,520,2048]{2,0,1:T(2,128)(2,1)} %copy.77), calls=%async_computation.2 | async-start | bytes 8519680 | tf_op jit(solution)/shard_map/all_to_all | solution.py:66
  154.6 387.7 %reduce-scatter.5.cloned.1.call-start = ((), (), s32[]{:S(2)}) async-start(), calls=%async_computation.7 | async-start | bytes 7864320 | tf_op jit(solution)/shard_map/reduce_scatter | solution.py:87
  263.0 1.1 copy-start.9
  263.0 19.8 %copy-start.6 = (bf16[2,520,768]{2,1,0:T(8,128)(2,1)}, bf16[2,520,768]{2,1,0:T(8,128)(2,1)S(1)}, u32[]{:S(2)}) copy-start(bf16[2,520,768]{2,1,0:T(8,128)(2,1)S(1)} %get-tuple-element.32) | copy-start | bytes 4792324
  282.8 262.2 %reduce-scatter.3.cloned.1.call-start = ((), (), s32[]{:S(2)}) async-start(), calls=%async_computation.6 | async-start | bytes 15728640 | tf_op jit(solution)/shard_map/reduce_scatter | solution.py:84
  312.6 4.9 copy-start.8
  312.6 100.3 %all-to-all-start.1 = ((bf16[2,520,2048]{2,0,1:T(2,128)(2,1)}), bf16[2,520,2048]{2,0,1:T(2,128)(2,1)}, u32[]{:S(2)}, u32[]{:S(2)}) async-start(bf16[2,520,2048]{2,0,1:T(2,128)(2,1)} %copy.74), calls=%async_computation.1 | async-start | bytes 8519680 | tf_op jit(solution)/shard_map/all_to_all | solution.py:72
  317.5 8.7 %copy-start.7 = (bf16[2,520,768]{2,1,0:T(8,128)(2,1)S(1)}, bf16[2,520,768]{2,1,0:T(8,128)(2,1)}, u32[]{:S(2)}) copy-start(bf16[2,520,768]{2,1,0:T(8,128)(2,1)} %copy-done.6) | copy-start | bytes 4792324
  412.9 100.2 %all-to-all-start.3 = ((bf16[2,520,2048]{2,0,1:T(2,128)(2,1)}), bf16[2,520,2048]{2,0,1:T(2,128)(2,1)}, u32[]{:S(2)}, u32[]{:S(2)}) async-start(bf16[2,520,2048]{2,0,1:T(2,128)(2,1)} %copy.79), calls=%async_computation.3 | async-start | bytes 8519680 | tf_op jit(solution)/shard_map/all_to_all | solution.py:73
  531.1 6.1 %copy-start.3 = (bf16[1024,2048]{1,0:T(8,128)(2,1)S(1)}, bf16[1024,2048]{1,0:T(8,128)(2,1)}, u32[]{:S(2)}) copy-start(bf16[1024,2048]{1,0:T(8,128)(2,1)} %gather_fusion.1) | copy-start | bytes 12582916
  531.1 6.0 %copy-start.5 = (f32[128,8]{1,0:T(8,128)S(1)}, f32[128,8]{1,0:T(8,128)}, u32[]{:S(2)}) copy-start(f32[128,8]{1,0:T(8,128)} %copy-done.4) | copy-start | bytes 12292
  542.3 6.4 %copy-start.1 = (bf16[128,2048]{1,0:T(8,128)(2,1)S(1)}, bf16[128,2048]{1,0:T(8,128)(2,1)}, u32[]{:S(2)}) copy-start(bf16[128,2048]{1,0:T(8,128)(2,1)} %param.7) | copy-start | bytes 1572868
Sparse Core Ops, SparseCore 0:
  282.9 69.0 reduce-scatter.4
  355.1 120.7 reduce-scatter.2
where the time goes:
time: 561 us; the launch traced here: 556 us
  waiting for transfers between devices  306 us (55%)
  matrix products  91.3 us (16%)
  local copies, waits for them, and re-layouts  85.1 us (15%)
  other arithmetic  37.7 us (7%)
  starting transfers between devices  21.3 us (4%)
  between operations  14.6 us (3%)
    all_to_all x1, waiting for transfers between devices, per_device(): lax.all_to_all(send_rows, 'expert', split_axis=1, concat_axis=1, tiled=True)  80.3 us
    all_to_all x1, waiting for transfers between devices, per_device(): lax.all_to_all(returned, 'expert', split_axis=1, concat_axis=1, tiled=True)  77.7 us
    all_to_all x1, waiting for transfers between devices, per_device(): lax.all_to_all(send_scaled, 'expert', split_axis=1, concat_axis=1, tiled=...  75.4 us
    all_to_all x1, waiting for transfers between devices, per_device(): lax.all_to_all(produced, 'expert', split_axis=1, concat_axis=1, tiled=True)  72.4 us
    select_n x1, other arithmetic, per_device(): jnp.where(filled[:, None], tokens[token_of], jnp.zeros((), jnp.bfloat16))  18.8 us
    dot_general x1, matrix products, per_device(): jnp.einsum('erd,erf->edf', scaled, hidden, preferred_element_type=jnp.flo...  18.6 us
    dot_general x1, matrix products, per_device(): jnp.einsum('erd,erf->edf', rows_in, grad_both, preferred_element_type=jnp...  16.2 us
    dot_general x1, matrix products, expert_pass(): jnp.einsum('erd,efd->erf', scaled, down_matrix, preferred_element_type=jn...  13 us
  transfers between devices with their start and end apart: 6, of which 4 were waited for; matrix products, arithmetic and copies ran while one was open for 25% of the time, Pallas kernels for 0%

commit v1 on v0

v1 whole, which is shorter than its diff:
```python
import jax
import jax.numpy as jnp
from jax import lax
from jax.sharding import PartitionSpec as P

F32 = jnp.float32
BF16 = jnp.bfloat16


def dot(a, b, ca, cb):
    return lax.dot_general(a, b, (((ca,), (cb,)), ((), ())), preferred_element_type=F32)


def per_device(tokens, routes, route_gates, gate_matrix, up_matrix, down_matrix, cotangent):
    homes, width, units = gate_matrix.shape
    first = lax.axis_index("expert") * homes
    all_tokens = lax.all_gather(tokens, "expert", axis=0, tiled=True)
    all_cot = lax.all_gather(cotangent, "expert", axis=0, tiled=True)
    all_routes = lax.all_gather(routes, "expert", axis=0, tiled=True)
    all_gates = lax.all_gather(route_gates, "expert", axis=0, tiled=True)

    hidden, grad_pre, grads = [], [], []
    for e in range(homes):
        weight = jnp.sum(jnp.where(all_routes == first + e, all_gates, 0.0), axis=1, keepdims=True)
        picked = jnp.any(all_routes == first + e, axis=1, keepdims=True)
        pre_gate = dot(all_tokens, gate_matrix[e], 1, 0)
        pre_up = dot(all_tokens, up_matrix[e], 1, 0)
        grad_hidden = dot(all_cot, down_matrix[e], 1, 1) * weight
        s = jax.nn.sigmoid(pre_gate)
        act = pre_gate * s
        hidden.append(jnp.where(picked, weight * act * pre_up, 0.0).astype(BF16))
        gpg = (grad_hidden * pre_up * s * (1.0 + pre_gate * (1.0 - s))).astype(BF16)
        gpu = (grad_hidden * act).astype(BF16)
        grad_pre.append((gpg, gpu))
    part_gate = jnp.stack([dot(all_tokens, g[0], 0, 0).astype(BF16) for g in grad_pre])
    part_up = jnp.stack([dot(all_tokens, g[1], 0, 0).astype(BF16) for g in grad_pre])
    part_down = jnp.stack([dot(h, all_cot, 0, 0).astype(BF16) for h in hidden])
    grad_gate = lax.psum_scatter(part_gate, "dp", scatter_dimension=1, tiled=True)
    grad_up = lax.psum_scatter(part_up, "dp", scatter_dimension=1, tiled=True)
    grad_down = lax.psum_scatter(part_down, "dp", scatter_dimension=2, tiled=True)
    out = sum(dot(h, down_matrix[e], 1, 0) for e, h in enumerate(hidden))
    back = sum(
        dot(g[0], gate_matrix[e], 1, 1) + dot(g[1], up_matrix[e], 1, 1)
        for e, g in enumerate(grad_pre)
    )
    layer_out = lax.psum_scatter(out.astype(BF16), "expert", scatter_dimension=0, tiled=True)
    grad_tokens = lax.psum_scatter(back.astype(BF16), "expert", scatter_dimension=0, tiled=True)
    return (layer_out, grad_tokens, grad_gate, grad_up, grad_down)


def solution(mesh):
    row = P(("dp", "expert"), None)
    home = P("expert", None, None)
    return jax.shard_map(
        per_device,
        mesh=mesh,
        in_specs=(row, row, row, home, home, home, row),
        out_specs=(row, row, P("expert", "dp", None), P("expert", "dp", None), P("expert", None, "dp")),
        check_vma=False,
    )
```

time: 561 us -> 470 us (0.84)
  local copies, waits for them, and re-layouts: 85.1 us -> 6.97 us
  blocking collectives: 0 us -> 30.1 us
  other arithmetic: 37.7 us -> 9.8 us
  matrix products: 91.3 us -> 119 us
  waiting for transfers between devices: 306 us -> 280 us
  starting transfers between devices: 21.3 us -> 0.28 us
    all_to_all x4 -> x0, waiting for transfers between devices: 306 us -> none  [the longest x1 80.3 us: per_device(): lax.all_to_all(send_rows, 'expert', split_axis=1, concat_axis=1, tiled=True)]
    reduce_scatter x2 -> x5, waiting for transfers between devices: 0.01 us -> 236 us  [the longest x1 72 us: per_device(): lax.psum_scatter(part_down, 'dp', scatter_dimension=2, tiled=True)]
    all_gather x0 -> x2, waiting for transfers between devices: none -> 42.6 us  [the longest x1 21.8 us: per_device(): all_cot = lax.all_gather(cotangent, 'expert', axis=0, tiled=True)]
    gather x5 -> x0, local copies, waits for them, and re-layouts: 39.4 us -> none  [the longest x1 11.9 us: per_device(): got_back.reshape(slot_count, width)[slot_of]]
    all_gather x0 -> x2, blocking collectives: none -> 30.1 us  [the longest x1 15.8 us: per_device(): all_routes = lax.all_gather(routes, 'expert', axis=0, tiled=True)]
    dot_general x8 -> x18, matrix products: 91.3 us -> 119 us  [dot(): lax.dot_general(a, b, (((ca,), (cb,)), ((), ())), preferred_element_type=...]
    all_to_all x4 -> x0, starting transfers between devices: 21 us -> none  [the longest x1 6.68 us: per_device(): lax.all_to_all(send_rows, 'expert', split_axis=1, concat_axis=1, tiled=True)]
    convert_element_type x3 -> x0, local copies, waits for them, and re-layouts: 19 us -> none  [the longest x1 6.37 us: per_device(): send_scaled = (gate_of[:, None] * cotangent[token_of].astype(jnp.float32)...]
  transfers between devices with their start and end apart: 6 -> 7, of which waited for: 4 -> 6; matrix products, arithmetic and copies ran while one was open for 25% -> 23% of each run, Pallas kernels for 0% -> 0%
where the time goes in v1:
time: 470 us; the launch traced here: 462 us
  waiting for transfers between devices  280 us (60%)
  matrix products  119 us (25%)
  blocking collectives  30.1 us (6%)
  between operations  14.8 us (3%)
  other arithmetic  9.8 us (2%)
  local copies, waits for them, and re-layouts  6.97 us (1%)
    dot_general x18, matrix products, dot(): lax.dot_general(a, b, (((ca,), (cb,)), ((), ())), preferred_element_type=...  119 us
    reduce_scatter x1, waiting for transfers between devices, per_device(): lax.psum_scatter(part_down, 'dp', scatter_dimension=2, tiled=True)  72 us
    reduce_scatter x1, waiting for transfers between devices, per_device(): lax.psum_scatter(part_gate, 'dp', scatter_dimension=1, tiled=True)  63.2 us
    reduce_scatter x1, waiting for transfers between devices, per_device(): lax.psum_scatter(out.astype(BF16), 'expert', scatter_dimension=0, tiled=T...  50.9 us
    reduce_scatter x1, waiting for transfers between devices, per_device(): lax.psum_scatter(back.astype(BF16), 'expert', scatter_dimension=0, tiled=...  50.2 us
    all_gather x1, waiting for transfers between devices, per_device(): all_cot = lax.all_gather(cotangent, 'expert', axis=0, tiled=True)  21.8 us
    all_gather x1, waiting for transfers between devices, per_device(): all_tokens = lax.all_gather(tokens, 'expert', axis=0, tiled=True)  20.9 us
    all_gather x1, blocking collectives, per_device(): all_routes = lax.all_gather(routes, 'expert', axis=0, tiled=True)  15.8 us
  transfers between devices with their start and end apart: 7, of which 6 were waited for; matrix products, arithmetic and copies ran while one was open for 23% of the time, Pallas kernels for 0%

profile of v1, /device:TPU:0, one launch (start us, length us, event | category | flops | bytes accessed | tf_op | source)
XLA Modules:
  0.0 461.7 jit_solution(8432220537915391508)
XLA Ops:
  7.2 0.0 all-gather.3.cloned.1.call-start
  7.2 0.7 all-gather.3.cloned.1.call-update
  7.9 0.0 all-gather.5.cloned.1.call-start
  7.9 0.7 all-gather.5.cloned.1.call-update
  8.6 0.0 reduce-scatter.12.cloned.1.call-start
  8.7 15.8 %all_gather.12 = s32[1024,8]{0,1:T(8,128)S(1)} all-gather(s32[128,8]{0,1:T(8,128)} %param.8), channel_id=1, replica_groups=mesh['dp'=4,'expert'=8] {'expert'}, dimensions={0}, use_global_device_ids=true | all-gather | bytes 36864 | tf_op jit(solution)/shard_map/all_gather | solution.py:19
  24.5 14.3 %all_gather.13 = f32[1024,8]{0,1:T(8,128)S(1)} all-gather(f32[128,8]{0,1:T(8,128)} %param.9), channel_id=1, replica_groups=mesh['dp'=4,'expert'=8] {'expert'}, dimensions={0}, use_global_device_ids=true | all-gather | bytes 36864 | tf_op jit(solution)/shard_map/all_gather | solution.py:20
  38.8 20.9 %all-gather.3.cloned.1.call-done = bf16[1024,2048]{1,0:T(8,128)(2,1)} async-done(((bf16[128,2048]{1,0:T(8,128)(2,1)}), bf16[1024,2048]{1,0:T(8,128)(2,1)}) %all-gather.3.cloned.1.call-update) | async-done | bytes 4194320 | tf_op jit(solution)/shard_map/all_gather | solution.py:17
  59.7 8.4 %fusion.4 = f32[1024,768]{1,0:T(8,128)} fusion(bf16[1024,2048]{1,0:T(8,128)(2,1)} %all-gather.3.cloned.1.call-done, bf16[2,2048,768]{2,1,0:T(8,128)(2,1)} %param.11), kind=kOutput, calls=%fused_computation.15 | convolution fusion | flops 3221225472 | bytes 10485760 | tf_op jit(solution)/shard_map/dot_general | solution.py:11
  68.1 7.2 %fusion.16 = f32[1024,768]{1,0:T(8,128)} fusion(bf16[1024,2048]{1,0:T(8,128)(2,1)S(1)} %copy-done.2, bf16[2,2048,768]{2,1,0:T(8,128)(2,1)} %param.11), kind=kOutput, calls=%fused_computation.27 | convolution fusion | flops 3221225472 | bytes 10485760 | tf_op jit(solution)/shard_map/dot_general | solution.py:11
  75.3 5.1 %fusion.8 = f32[1024,768]{1,0:T(8,128)} fusion(bf16[1024,2048]{1,0:T(8,128)(2,1)S(1)} %copy-done.2, bf16[2,2048,768]{2,1,0:T(8,128)(2,1)S(1)} %bitcast.79), kind=kOutput, calls=%fused_computation.19 | convolution fusion | flops 3221225472 | bytes 10485760 | tf_op jit(solution)/shard_map/dot_general | solution.py:11
  80.4 5.1 %fusion.20 = f32[1024,768]{1,0:T(8,128)} fusion(bf16[1024,2048]{1,0:T(8,128)(2,1)S(1)} %copy-done.2, bf16[2,2048,768]{2,1,0:T(8,128)(2,1)S(1)} %bitcast.79), kind=kOutput, calls=%fused_computation.31 | convolution fusion | flops 3221225472 | bytes 10485760 | tf_op jit(solution)/shard_map/dot_general | solution.py:11
  85.5 21.8 %all-gather.5.cloned.1.call-done = bf16[1024,2048]{1,0:T(8,128)(2,1)} async-done(((bf16[128,2048]{1,0:T(8,128)(2,1)}), bf16[1024,2048]{1,0:T(8,128)(2,1)}) %all-gather.5.cloned.1.call-update) | async-done | bytes 4194320 | tf_op jit(solution)/shard_map/all_gather | solution.py:18
  107.3 10.1 %multiply_convert_fusion = (bf16[1024,768]{1,0:T(8,128)(2,1)S(1)}, bf16[1024,768]{1,0:T(8,128)(2,1)}, bf16[1024,768]{1,0:T(8,128)(2,1)S(1)}) fusion(f32[1024]{0:T(1024)S(1)} %get-tuple-element.10, f32[1024,768]{1,0:T(8,128)} %fusion.8, f32[1024,768]{1,0:T(8,128)} %fusion.4, pred[1024]{0:T(1024)(128)(4,1)S(1)} %get-tuple-element.22, ...), kind=kOutput, calls=%fused_computation.33 | convolution fusion | flops 3235381248 | bytes 18355200 | tf_op jit(solution)/shard_map/dot_general | solution.py:11
  117.4 3.7 fusion.27
  121.1 0.3 copy-done.11
  121.4 8.2 %multiply_convert_fusion.2 = (bf16[1024,768]{1,0:T(8,128)(2,1)S(1)}, bf16[1024,768]{1,0:T(8,128)(2,1)}, bf16[1024,768]{1,0:T(8,128)(2,1)}) fusion(f32[1024]{0:T(1024)S(1)} %get-tuple-element.11, f32[1024,768]{1,0:T(8,128)S(1)} %copy-done.11, f32[1024,768]{1,0:T(8,128)S(1)} %copy-done.10, pred[1024]{0:T(1024)(128)(4,1)S(1)} %get-tuple-element.14, ...), kind=kOutput, calls=%fused_computation.35 | convolution fusion | flops 3235381248 | bytes 18355200 | tf_op jit(solution)/shard_map/dot_general | solution.py:11
  129.7 3.7 fusion.26
  133.4 3.3 pad_maximum_fusion.1
  136.6 0.0 reduce-scatter.12.cloned.1.call-update
  136.7 0.0 reduce-scatter.10.cloned.1.call-start
  136.7 6.3 %fusion.25 = bf16[1,2048,768]{1,2,0:T(8,128)(2,1)S(1)} fusion(bf16[1024,768]{1,0:T(8,128)(2,1)} %get-tuple-element.17, bf16[1024,2048]{1,0:T(8,128)(2,1)} %all-gather.3.cloned.1.call-done), kind=kOutput, calls=%fused_computation.44 | convolution fusion | flops 3222798336 | bytes 8912896 | tf_op jit(solution)/shard_map/dot_general | solution.py:11
  143.0 3.9 fusion.24
  147.0 3.3 pad_maximum_fusion
  150.3 0.0 reduce-scatter.10.cloned.1.call-update
  150.3 0.0 reduce-scatter.8.cloned.1.call-start
  150.4 9.2 %fusion.18 = f32[1024,2048]{1,0:T(8,128)} fusion(bf16[1024,768]{1,0:T(8,128)(2,1)} %get-tuple-element.20, bf16[2,2048,768]{2,1,0:T(8,128)(2,1)} %param.10), kind=kOutput, calls=%fused_computation.29 | convolution fusion | flops 3221225472 | bytes 13107200 | tf_op jit(solution)/shard_map/dot_general | solution.py:11
  159.6 7.7 %fusion.14 = f32[1024,2048]{1,0:T(8,128)} fusion(bf16[1024,768]{1,0:T(8,128)(2,1)S(1)} %copy-done.8, bf16[2,2048,768]{2,1,0:T(8,128)(2,1)} %param.11), kind=kOutput, calls=%fused_computation.25 | convolution fusion | flops 3221225472 | bytes 13107200 | tf_op jit(solution)/shard_map/dot_general | solution.py:11
  167.3 5.7 %fusion.6 = f32[1024,2048]{1,0:T(8,128)} fusion(bf16[1024,768]{1,0:T(8,128)(2,1)S(1)} %copy-done.6, bf16[2,2048,768]{2,1,0:T(8,128)(2,1)S(1)} %bitcast.81), kind=kOutput, calls=%fused_computation.17 | convolution fusion | flops 3221225472 | bytes 13107200 | tf_op jit(solution)/shard_map/dot_general | solution.py:11
  173.1 12.7 %add_convert_fusion = bf16[1024,2048]{1,0:T(8,128)(2,1)} fusion(f32[1024,2048]{1,0:T(8,128)} %fusion.6, f32[1024,2048]{1,0:T(8,128)} %fusion.18, f32[1024,2048]{1,0:T(8,128)} %fusion.14, bf16[1024,768]{1,0:T(8,128)(2,1)S(1)} %get-tuple-element.16, bf16[2,2048,768]{2,1,0:T(8,128)(2,1)} %param.11), kind=kOutput, calls=%fused_computation | convolution fusion | flops 3229614080 | bytes 34078720 | tf_op jit(solution)/shard_map/dot_general | solution.py:11
  185.8 0.0 reduce-scatter.8.cloned.1.call-update
  185.8 0.0 reduce-scatter.6.cloned.1.call-start
  185.8 1.4 copy-done.5
  187.3 5.3 %fusion.12 = f32[1024,2048]{1,0:T(8,128)S(1)} fusion(bf16[1024,768]{1,0:T(8,128)(2,1)S(1)} %copy-done.5, bf16[2,768,2048]{2,1,0:T(8,128)(2,1)} %param.12), kind=kOutput, calls=%fused_computation.23 | convolution fusion | flops 3221225472 | bytes 13107200 | tf_op jit(solution)/shard_map/dot_general | solution.py:11
  192.6 7.0 %add_convert_fusion.1 = bf16[1024,2048]{1,0:T(8,128)(2,1)} fusion(f32[1024,2048]{1,0:T(8,128)S(1)} %fusion.12, bf16[1024,768]{1,0:T(8,128)(2,1)S(1)} %get-tuple-element.18, bf16[2,768,2048]{2,1,0:T(8,128)(2,1)} %param.12), kind=kOutput, calls=%fused_computation.1 | convolution fusion | flops 3225419776 | bytes 17301504 | tf_op jit(solution)/shard_map/dot_general | solution.py:11
  199.6 0.0 reduce-scatter.6.cloned.1.call-update
  199.6 0.0 reduce-scatter.14.cloned.1.call-start
  199.6 6.4 %fusion.29 = bf16[1,768,2048]{2,1,0:T(8,128)(2,1)S(1)} fusion(bf16[1024,768]{1,0:T(8,128)(2,1)S(1)} %get-tuple-element.18, bf16[1024,2048]{1,0:T(8,128)(2,1)} %all-gather.5.cloned.1.call-done), kind=kOutput, calls=%fused_computation.48 | convolution fusion | flops 3222798336 | bytes 8912896 | tf_op jit(solution)/shard_map/dot_general | solution.py:11
  206.1 3.7 fusion.28
  209.8 3.2 pad_maximum_fusion.2
  213.0 0.0 reduce-scatter.14.cloned.1.call-update
  213.0 0.0 reduce-scatter.12.cloned.1.call-done
  213.0 2.6 copy.13
  215.6 63.2 %reduce-scatter.10.cloned.1.call-done = bf16[2,512,768]{1,2,0:T(8,128)(2,1)} async-done(((bf16[2,2048,768]{1,2,0:T(8,128)(2,1)}), bf16[2,512,768]{1,2,0:T(8,128)(2,1)}) %reduce-scatter.10.cloned.1.call-update) | async-done | bytes 1572880 | tf_op jit(solution)/shard_map/reduce_scatter | solution.py:38
  278.8 2.6 copy.12
  281.4 50.2 %reduce-scatter.8.cloned.1.call-done = bf16[128,2048]{1,0:T(8,128)(2,1)} async-done(((bf16[1024,2048]{1,0:T(8,128)(2,1)}), bf16[128,2048]{1,0:T(8,128)(2,1)}) %reduce-scatter.8.cloned.1.call-update) | async-done | bytes 524304 | tf_op jit(solution)/shard_map/reduce_scatter | solution.py:47
  331.6 50.9 %reduce-scatter.6.cloned.1.call-done = bf16[128,2048]{1,0:T(8,128)(2,1)} async-done(((bf16[1024,2048]{1,0:T(8,128)(2,1)}), bf16[128,2048]{1,0:T(8,128)(2,1)}) %reduce-scatter.6.cloned.1.call-update) | async-done | bytes 524304 | tf_op jit(solution)/shard_map/reduce_scatter | solution.py:46
  382.5 72.0 %reduce-scatter.14.cloned.1.call-done = bf16[2,768,512]{2,1,0:T(8,128)(2,1)} async-done(((bf16[2,768,2048]{2,1,0:T(8,128)(2,1)}), bf16[2,768,512]{2,1,0:T(8,128)(2,1)}) %reduce-scatter.14.cloned.1.call-update) | async-done | bytes 1572880 | tf_op jit(solution)/shard_map/reduce_scatter | solution.py:40
  (34 shorter events, 0.1 us)
Async XLA Ops:
  7.2 52.5 %all-gather.3.cloned.1.call-start = ((), (), s32[]{:S(2)}) async-start(), calls=%async_computation.5 | async-start | bytes 4718592 | tf_op jit(solution)/shard_map/all_gather | solution.py:17
  7.9 99.4 %all-gather.5.cloned.1.call-start = ((), (), s32[]{:S(2)}) async-start(), calls=%async_computation.7 | async-start | bytes 4718592 | tf_op jit(solution)/shard_map/all_gather | solution.py:18
  8.6 204.4 %reduce-scatter.12.cloned.1.call-start = ((), (), s32[]{:S(2)}) async-start(), calls=%async_computation.10 | async-start | bytes 7864320 | tf_op jit(solution)/shard_map/reduce_scatter | solution.py:39
  59.7 8.4 %copy-start.2 = (bf16[1024,2048]{1,0:T(8,128)(2,1)S(1)}, bf16[1024,2048]{1,0:T(8,128)(2,1)}, u32[]{:S(2)}) copy-start(bf16[1024,2048]{1,0:T(8,128)(2,1)} %all-gather.3.cloned.1.call-done) | copy-start | bytes 12582916
  59.7 15.6 %slice-start = ((s8[6291456]{0:T(1024)(128)(4,1)}), s8[4194304]{0:T(1024)(128)(4,1)S(1)}, s32[]{:S(2)}) async-start(s8[6291456]{0:T(1024)(128)(4,1)} %bitcast.78), calls=%async_computation.12 | async-start | bytes 8388608
  68.1 7.2 %slice-start.1 = ((s8[6291456]{0:T(1024)(128)(4,1)}), s8[2097152]{0:T(1024)(128)(4,1)S(1)}, s32[]{:S(2)}) async-start(s8[6291456]{0:T(1024)(128)(4,1)} %bitcast.78), calls=%async_computation.13 | async-start | bytes 4194304
  107.3 10.1 %copy-start.3 = (bf16[1024,2048]{1,0:T(8,128)(2,1)S(1)}, bf16[1024,2048]{1,0:T(8,128)(2,1)}, u32[]{:S(2)}) copy-start(bf16[1024,2048]{1,0:T(8,128)(2,1)} %all-gather.3.cloned.1.call-done) | copy-start | bytes 12582916
  117.4 3.7 copy-start
  117.4 3.7 copy-start.10
  117.4 4.1 copy-start.11
  129.7 3.7 copy-start.7
  136.7 142.1 %reduce-scatter.10.cloned.1.call-start = ((), (), s32[]{:S(2)}) async-start(), calls=%async_computation.9 | async-start | bytes 7864320 | tf_op jit(solution)/shard_map/reduce_scatter | solution.py:38
  136.7 6.3 %copy-start.4 = (bf16[1024,2048]{1,0:T(8,128)(2,1)S(1)}, bf16[1024,2048]{1,0:T(8,128)(2,1)}, u32[]{:S(2)}) copy-start(bf16[1024,2048]{1,0:T(8,128)(2,1)} %all-gather.3.cloned.1.call-done) | copy-start | bytes 12582916
  136.7 6.3 %copy-start.9 = (bf16[1024,768]{1,0:T(8,128)(2,1)S(1)}, bf16[1024,768]{1,0:T(8,128)(2,1)}, u32[]{:S(2)}) copy-start(bf16[1024,768]{1,0:T(8,128)(2,1)} %get-tuple-element.20) | copy-start | bytes 4718596
  150.3 181.3 %reduce-scatter.8.cloned.1.call-start = ((), (), s32[]{:S(2)}) async-start(), calls=%async_computation.8 | async-start | bytes 4718592 | tf_op jit(solution)/shard_map/reduce_scatter | solution.py:47
  150.3 9.2 %copy-start.8 = (bf16[1024,768]{1,0:T(8,128)(2,1)S(1)}, bf16[1024,768]{1,0:T(8,128)(2,1)}, u32[]{:S(2)}) copy-start(bf16[1024,768]{1,0:T(8,128)(2,1)} %copy-done.7) | copy-start | bytes 4718596
  150.4 16.9 %slice-start.2 = ((s8[6291456]{0:T(1024)(128)(4,1)}), s8[4194304]{0:T(1024)(128)(4,1)S(1)}, s32[]{:S(2)}) async-start(s8[6291456]{0:T(1024)(128)(4,1)} %bitcast.80), calls=%async_computation.14 | async-start | bytes 8388608
  159.6 7.7 %slice-start.3 = ((s8[6291456]{0:T(1024)(128)(4,1)}), s8[2097152]{0:T(1024)(128)(4,1)S(1)}, s32[]{:S(2)}) async-start(s8[6291456]{0:T(1024)(128)(4,1)} %bitcast.80), calls=%async_computation.15 | async-start | bytes 4194304
  159.6 7.7 %copy-start.6 = (bf16[1024,768]{1,0:T(8,128)(2,1)S(1)}, bf16[1024,768]{1,0:T(8,128)(2,1)}, u32[]{:S(2)}) copy-start(bf16[1024,768]{1,0:T(8,128)(2,1)} %get-tuple-element.17) | copy-start | bytes 4718596
  185.8 1.5 copy-start.5
  185.8 196.7 %reduce-scatter.6.cloned.1.call-start = ((), (), s32[]{:S(2)}) async-start(), calls=%async_computation.6 | async-start | bytes 4718592 | tf_op jit(solution)/shard_map/reduce_scatter | solution.py:46
  199.6 254.8 %reduce-scatter.14.cloned.1.call-start = ((), (), s32[]{:S(2)}) async-start(), calls=%async_computation.11 | async-start | bytes 7864320 | tf_op jit(solution)/shard_map/reduce_scatter | solution.py:40
  199.6 6.4 %copy-start.1 = (bf16[1024,2048]{1,0:T(8,128)(2,1)S(1)}, bf16[1024,2048]{1,0:T(8,128)(2,1)}, u32[]{:S(2)}) copy-start(bf16[1024,2048]{1,0:T(8,128)(2,1)} %all-gather.5.cloned.1.call-done) | copy-start | bytes 12582916
Sparse Core Ops, SparseCore 0:
  9.6 50.0 all-gather.2
  61.3 45.9 all-gather.4
  136.8 68.9 reduce-scatter.11
  208.6 70.1 reduce-scatter.9
  281.5 50.0 reduce-scatter.7
  334.3 48.1 reduce-scatter.5
  386.0 68.3 reduce-scatter.13

commit v2 on v1

v2 whole, which is shorter than its diff:
```python
import functools

import jax
import jax.numpy as jnp
from jax import lax
from jax.experimental import pallas as pl
from jax.experimental.pallas import tpu as pltpu
from jax.sharding import PartitionSpec as P

F32 = jnp.float32
BF16 = jnp.bfloat16
MIB = 1 << 20


def dot(a, b, ca, cb):
    return lax.dot_general(a, b, (((ca,), (cb,)), ((), ())), preferred_element_type=F32)


def outputs_kernel(homes, *refs):
    gpg, gpu, hid = refs[:homes], refs[homes : 2 * homes], refs[2 * homes : 3 * homes]
    gate, up, down, out, back = refs[3 * homes :]
    acc = dot(hid[0][...], down[0], 1, 0)
    for e in range(1, homes):
        acc += dot(hid[e][...], down[e], 1, 0)
    out[...] = acc.astype(BF16)
    acc = dot(gpg[0][...], gate[0], 1, 1) + dot(gpu[0][...], up[0], 1, 1)
    for e in range(1, homes):
        acc += dot(gpg[e][...], gate[e], 1, 1) + dot(gpu[e][...], up[e], 1, 1)
    back[...] = acc.astype(BF16)


def outputs_call(factors, gate_matrix, up_matrix, down_matrix):
    homes, width, units = gate_matrix.shape
    rows = factors[0].shape[0]
    tile = 256
    whole = pl.BlockSpec((rows, units), lambda i: (0, 0))
    by_row = pl.BlockSpec((homes, tile, units), lambda i: (0, i, 0))
    by_col = pl.BlockSpec((homes, units, tile), lambda i: (0, 0, i))
    flops = 2 * rows * units * width * 3 * homes
    return pl.pallas_call(
        functools.partial(outputs_kernel, homes),
        grid=(width // tile,),
        out_shape=[jax.ShapeDtypeStruct((rows, width), BF16)] * 2,
        in_specs=[whole] * (3 * homes) + [by_row, by_row, by_col],
        out_specs=[pl.BlockSpec((rows, tile), lambda i: (0, i))] * 2,
        compiler_params=pltpu.CompilerParams(vmem_limit_bytes=56 * MIB),
        cost_estimate=pl.CostEstimate(flops=flops, bytes_accessed=36 * MIB, transcendentals=0),
    )(*factors, gate_matrix, up_matrix, down_matrix)


def grads_kernel(count, cols, tok_hbm, cot_hbm, *refs):
    factor_hbm = refs[:count]
    (out, both, factor, turned, stage, relay, land, in_sem, send_sem, relay_sem, land_sem) = refs[count:]
    split = 2 * count // 3
    me = lax.axis_index("dp")
    near_a = me + 1 - 2 * (me % 2)
    near_b = me + 2 - 4 * (me // 2)
    far = 3 - me

    loads = [pltpu.make_async_copy(tok_hbm, both.at[0], in_sem.at[0])]
    loads += [pltpu.make_async_copy(cot_hbm, both.at[1], in_sem.at[1])]
    loads += [
        pltpu.make_async_copy(factor_hbm[j], factor.at[j], in_sem.at[2 + j]) for j in range(count)
    ]
    for load in loads:
        load.start()
    barrier = pltpu.get_barrier_semaphore()
    for peer in (near_a, near_b):
        pl.semaphore_signal(
            barrier, inc=1, device_id={"dp": peer}, device_id_type=pl.DeviceIdType.MESH
        )
    pl.semaphore_wait(barrier, 2)
    for load in loads:
        load.wait()

    def remote(src, dst, send, recv, peer):
        return pltpu.make_async_remote_copy(
            src_ref=src,
            dst_ref=dst,
            send_sem=send,
            recv_sem=recv,
            device_id={"dp": peer},
            device_id_type=pl.DeviceIdType.MESH,
        )

    def to_relay(j, peer):
        return remote(stage.at[0, j], relay.at[j], send_sem.at[0, j], relay_sem.at[j], peer)

    def to_land(way, j, peer):
        return remote(
            stage.at[1 + way, j], land.at[way, j], send_sem.at[1 + way, j], land_sem.at[way, j], peer
        )

    def turn(owner):
        start = pl.multiple_of(owner * cols, cols)
        for side in range(2):
            turned[side] = both[side, :, pl.ds(start, cols)].T

    def chunk(j):
        return dot(turned[j // split], factor[j], 1, 0).astype(BF16)

    pairs = count // 2
    turn(far)

    @pl.loop(0, pairs)
    def _(k):
        for side, peer in ((0, near_a), (1, near_b)):
            j = 2 * k + side
            stage[0, j] = chunk(j)
            to_relay(j, peer).start()

    for way, peer in ((0, near_a), (1, near_b)):
        turn(peer)

        @pl.loop(0, pairs)
        def _(k, way=way, peer=peer):
            j = 2 * k + way
            stage[1 + way, j] = chunk(j)
            to_land(way, j, peer).start()
            other = 2 * k + 1 - way
            stage[1 + way, other] = chunk(other)

    turn(me)

    @pl.loop(0, count)
    def _(j):
        out[j] = chunk(j)

    @pl.loop(0, pairs)
    def _(k):
        for side, peer in ((0, near_a), (1, near_b)):
            j, way = 2 * k + side, 1 - side
            to_relay(j, peer).wait_recv()
            stage[1 + way, j] = (stage[1 + way, j].astype(F32) + relay[j].astype(F32)).astype(BF16)
            to_land(way, j, near_b if way else near_a).start()

    @pl.loop(0, count)
    def _(j):
        to_land(0, j, near_a).wait_recv()
        to_land(1, j, near_b).wait_recv()
        total = out[j].astype(F32) + land[0, j].astype(F32) + land[1, j].astype(F32)
        out[j] = total.astype(BF16)

    @pl.loop(0, count)
    def _(j):
        to_relay(j, near_a).wait_send()
        to_land(0, j, near_a).wait_send()
        to_land(1, j, near_b).wait_send()


def grads_call(all_tokens, all_cot, factors):
    rows, width = all_tokens.shape
    units = factors[0].shape[1]
    count = len(factors)
    cols = width // lax.axis_size("dp")
    piece = (cols, units)
    dma = pltpu.SemaphoreType.DMA
    return pl.pallas_call(
        functools.partial(grads_kernel, count, cols),
        out_shape=jax.ShapeDtypeStruct((count,) + piece, BF16),
        in_specs=[pl.BlockSpec(memory_space=pl.ANY)] * (2 + count),
        out_specs=pl.BlockSpec(memory_space=pltpu.VMEM),
        scratch_shapes=[
            pltpu.VMEM((2, rows, width), BF16),
            pltpu.VMEM((count, rows, units), BF16),
            pltpu.VMEM((2, cols, rows), BF16),
            pltpu.VMEM((3, count) + piece, BF16),
            pltpu.VMEM((count,) + piece, BF16),
            pltpu.VMEM((2, count) + piece, BF16),
            dma((2 + count,)),
            dma((3, count)),
            dma((count,)),
            dma((2, count)),
        ],
        compiler_params=pltpu.CompilerParams(
            collective_id=0, has_side_effects=True, vmem_limit_bytes=60 * MIB
        ),
        cost_estimate=pl.CostEstimate(
            flops=2 * rows * width * units * count * 8, bytes_accessed=24 * MIB, transcendentals=0
        ),
    )(all_tokens, all_cot, *factors)


def per_device(tokens, routes, route_gates, gate_matrix, up_matrix, down_matrix, cotangent):
    homes, width, units = gate_matrix.shape
    first = lax.axis_index("expert") * homes
    all_tokens = lax.all_gather(tokens, "expert", axis=0, tiled=True)
    all_cot = lax.all_gather(cotangent, "expert", axis=0, tiled=True)
    all_routes = lax.all_gather(routes, "expert", axis=0, tiled=True)
    all_gates = lax.all_gather(route_gates, "expert", axis=0, tiled=True)
    rows = all_tokens.shape[0]
    kernels = rows * (2 * width + 3 * homes * units) * 2 <= 18 * MIB and lax.axis_size("dp") == 4

    hidden, gpgs, gpus = [], [], []
    for e in range(homes):
        weight = jnp.sum(jnp.where(all_routes == first + e, all_gates, 0.0), axis=1, keepdims=True)
        pre_gate = dot(all_tokens, gate_matrix[e], 1, 0)
        pre_up = dot(all_tokens, up_matrix[e], 1, 0)
        grad_hidden = dot(all_cot, down_matrix[e], 1, 1) * weight
        s = jax.nn.sigmoid(pre_gate)
        act = pre_gate * s
        hidden.append((weight * act * pre_up).astype(BF16))
        gpgs.append((grad_hidden * pre_up * s * (1.0 + pre_gate * (1.0 - s))).astype(BF16))
        gpus.append((grad_hidden * act).astype(BF16))

    if kernels:
        factors = gpgs + gpus + hidden
        out, back = outputs_call(factors, gate_matrix, up_matrix, down_matrix)
        factors, out, back = lax.optimization_barrier((factors, out, back))
        summed = grads_call(all_tokens, all_cot, factors)
        grad_gate, grad_up = summed[:homes], summed[homes : 2 * homes]
        grad_down = jnp.swapaxes(summed[2 * homes :], 1, 2)
    else:
        part_gate = jnp.stack([dot(all_tokens, g, 0, 0).astype(BF16) for g in gpgs])
        part_up = jnp.stack([dot(all_tokens, g, 0, 0).astype(BF16) for g in gpus])
        part_down = jnp.stack([dot(h, all_cot, 0, 0).astype(BF16) for h in hidden])
        grad_gate = lax.psum_scatter(part_gate, "dp", scatter_dimension=1, tiled=True)
        grad_up = lax.psum_scatter(part_up, "dp", scatter_dimension=1, tiled=True)
        grad_down = lax.psum_scatter(part_down, "dp", scatter_dimension=2, tiled=True)
        out = sum(dot(h, down_matrix[e], 1, 0) for e, h in enumerate(hidden)).astype(BF16)
        back = sum(
            dot(gpgs[e], gate_matrix[e], 1, 1) + dot(gpus[e], up_matrix[e], 1, 1)
            for e in range(homes)
        ).astype(BF16)
    layer_out = lax.psum_scatter(out, "expert", scatter_dimension=0, tiled=True)
    grad_tokens = lax.psum_scatter(back, "expert", scatter_dimension=0, tiled=True)
    return (layer_out, grad_tokens, grad_gate, grad_up, grad_down)


def solution(mesh):
    row = P(("dp", "expert"), None)
    home = P("expert", None, None)
    return jax.shard_map(
        per_device,
        mesh=mesh,
        in_specs=(row, row, row, home, home, home, row),
        out_specs=(row, row, P("expert", "dp", None), P("expert", "dp", None), P("expert", None, "dp")),
        check_vma=False,
    )
```

time: 470 us -> 339 us (0.72); the launches traced: 462 us -> 338 us
  waiting for transfers between devices: 280 us -> 56.5 us
  Pallas kernels: 0 us -> 194 us
  matrix products: 119 us -> 38.2 us
  other arithmetic: 9.8 us -> 0.02 us
    reduce_scatter x5 -> x2, waiting for transfers between devices: 236 us -> 0.01 us  [the longest x1 0.01 us: per_device(): layer_out = lax.psum_scatter(out, 'expert', scatter_dimension=0, tiled=True)]
    pallas_call x0 -> x2, Pallas kernels: none -> 194 us  [the longest x1 167 us: grads_call(): pl.pallas_call(functools.partial(grads_kernel, count, cols), out_shape=ja...]
    dot_general x18 -> x6, matrix products: 119 us -> 38.2 us  [dot(): lax.dot_general(a, b, (((ca,), (cb,)), ((), ())), preferred_element_type=...]
    all_gather x1, waiting for transfers between devices: 21.8 us -> 33.7 us  [per_device(): all_cot = lax.all_gather(cotangent, 'expert', axis=0, tiled=True)]
    another operation x3 -> x0, other arithmetic: 9.73 us -> none  [the longest x1 3.28 us: per_device(): jnp.stack([dot(all_tokens, g[0], 0, 0).astype(BF16) for g in grad_pre])]
    unnamed x34 -> x13, local copies, waits for them, and re-layouts: 6.97 us -> 1.6 us
  transfers between devices with their start and end apart: 7 -> 4, of which waited for: 6 -> 2; matrix products, arithmetic and copies ran while one was open for 23% -> 6% of each run, Pallas kernels for 0% -> 49%
where the time goes in v2:
time: 339 us; the launch traced here: 338 us
  Pallas kernels  194 us (57%)
  waiting for transfers between devices  56.5 us (17%)
  matrix products  38.2 us (11%)
  blocking collectives  30.1 us (9%)
  between operations  13.9 us (4%)
  local copies, waits for them, and re-layouts  5.92 us (2%)
    pallas_call x1, Pallas kernels, grads_call(): pl.pallas_call(functools.partial(grads_kernel, count, cols), out_shape=ja...  167 us
    dot_general x6, matrix products, dot(): lax.dot_general(a, b, (((ca,), (cb,)), ((), ())), preferred_element_type=...  38.2 us
    all_gather x1, waiting for transfers between devices, per_device(): all_cot = lax.all_gather(cotangent, 'expert', axis=0, tiled=True)  33.7 us
    pallas_call x1, Pallas kernels, outputs_call(): pl.pallas_call(functools.partial(outputs_kernel, homes), grid=(width // t...  26.5 us
    all_gather x1, waiting for transfers between devices, per_device(): all_tokens = lax.all_gather(tokens, 'expert', axis=0, tiled=True)  20.9 us
    all_gather x1, blocking collectives, per_device(): all_gates = lax.all_gather(route_gates, 'expert', axis=0, tiled=True)  15.8 us
    all_gather x1, blocking collectives, per_device(): all_routes = lax.all_gather(routes, 'expert', axis=0, tiled=True)  14.3 us
  transfers between devices with their start and end apart: 4, of which 2 were waited for; matrix products, arithmetic and copies ran while one was open for 6% of the time, Pallas kernels for 49%

profile of v2, /device:TPU:0, one launch (start us, length us, event | category | flops | bytes accessed | tf_op | source)
XLA Modules:
  0.0 338.5 jit_solution(17010438895868545655)
XLA Ops:
  7.2 0.0 all-gather.5.cloned.1.call-start
  7.2 0.7 all-gather.5.cloned.1.call-update
  7.9 0.0 all-gather.3.cloned.1.call-start
  7.9 0.7 all-gather.3.cloned.1.call-update
  8.6 0.0 reduce-scatter.3.cloned.1.call-start
  8.7 15.8 %all_gather.14 = f32[1024,8]{0,1:T(8,128)S(1)} all-gather(f32[128,8]{0,1:T(8,128)} %param.9), channel_id=1, replica_groups=mesh['dp'=4,'expert'=8] {'expert'}, dimensions={0}, use_global_device_ids=true | all-gather | bytes 36864 | tf_op jit(solution)/shard_map/all_gather | solution.py:190
  24.5 14.3 %all_gather.13 = s32[1024,8]{0,1:T(8,128)S(1)} all-gather(s32[128,8]{0,1:T(8,128)} %param.8), channel_id=1, replica_groups=mesh['dp'=4,'expert'=8] {'expert'}, dimensions={0}, use_global_device_ids=true | all-gather | bytes 36864 | tf_op jit(solution)/shard_map/all_gather | solution.py:189
  38.8 20.9 %all-gather.5.cloned.1.call-done.tok_hbm = bf16[1024,2048]{1,0:T(8,128)(2,1)} async-done(((bf16[128,2048]{1,0:T(8,128)(2,1)}), bf16[1024,2048]{1,0:T(8,128)(2,1)}) %all-gather.5.cloned.1.call-update) | async-done | bytes 4194320 | tf_op jit(solution)/shard_map/all_gather | solution.py:187
  59.7 0.0 copy-start
  59.7 8.3 %fusion.6 = f32[1024,768]{1,0:T(8,128)} fusion(bf16[1024,2048]{1,0:T(8,128)(2,1)} %all-gather.5.cloned.1.call-done.tok_hbm, bf16[2,2048,768]{2,1,0:T(8,128)(2,1)} %refs_6_.1), kind=kOutput, calls=%fused_computation.6 | convolution fusion | flops 3221225472 | bytes 10485760 | tf_op jit(solution)/shard_map/dot_general | solution.py:16
  68.0 0.0 copy-done
  68.0 5.6 %fusion = f32[1024,768]{1,0:T(8,128)S(1)} fusion(bf16[1024,2048]{1,0:T(8,128)(2,1)S(1)} %copy-done, bf16[2,2048,768]{2,1,0:T(8,128)(2,1)} %refs_6_.1), kind=kOutput, calls=%fused_computation | convolution fusion | flops 3221225472 | bytes 10485760 | tf_op jit(solution)/shard_map/dot_general | solution.py:16
  73.6 33.7 %all-gather.3.cloned.1.call-done.cot_hbm = bf16[1024,2048]{1,0:T(8,128)(2,1)} async-done(((bf16[128,2048]{1,0:T(8,128)(2,1)}), bf16[1024,2048]{1,0:T(8,128)(2,1)}) %all-gather.3.cloned.1.call-update) | async-done | bytes 4194320 | tf_op jit(solution)/shard_map/all_gather | solution.py:188
  107.3 0.0 copy-start.2
  107.3 0.0 slice-start
  107.3 6.4 %fusion.10 = f32[1024,768]{1,0:T(8,128)S(1)} fusion(bf16[1024,2048]{1,0:T(8,128)(2,1)} %all-gather.3.cloned.1.call-done.cot_hbm, bf16[2,768,2048]{2,1,0:T(8,128)(2,1)} %refs_8_.1), kind=kOutput, calls=%fused_computation.10 | convolution fusion | flops 3221225472 | bytes 10485760 | tf_op jit(solution)/shard_map/dot_general | solution.py:16
  113.7 0.0 copy-done.2
  113.7 0.0 slice-start.1
  113.7 0.0 copy-start.1
  113.7 0.0 copy-start.3
  113.7 5.5 %fusion.4 = f32[1024,768]{1,0:T(8,128)S(1)} fusion(bf16[1024,2048]{1,0:T(8,128)(2,1)S(1)} %copy-done.2, bf16[2,768,2048]{2,1,0:T(8,128)(2,1)} %refs_8_.1), kind=kOutput, calls=%fused_computation.4 | convolution fusion | flops 3221225472 | bytes 10485760 | tf_op jit(solution)/shard_map/dot_general | solution.py:16
  119.2 0.0 slice-done
  119.2 0.0 slice-done.1
  119.2 0.0 copy-done.1
  119.2 0.0 copy-done.3
  119.2 6.2 %multiply_convert_fusion.1 = (bf16[1024,768]{1,0:T(8,128)(2,1)}, bf16[1024,768]{1,0:T(8,128)(2,1)}, bf16[1024,768]{1,0:T(8,128)(2,1)}) fusion(f32[1024]{0:T(1024)S(1)} %get-tuple-element.31, f32[1024,768]{1,0:T(8,128)S(1)} %copy-done.3, f32[1024,768]{1,0:T(8,128)S(1)} %fusion.10, bf16[1024,2048]{1,0:T(8,128)(2,1)S(1)} %copy-done.1, ...), kind=kOutput, calls=%fused_computation.13 | convolution fusion | flops 3234594816 | bytes 18354176 | tf_op jit(solution)/shard_map/dot_general | solution.py:16
  125.4 6.3 %multiply_convert_fusion = (bf16[1024,768]{1,0:T(8,128)(2,1)}, bf16[1024,768]{1,0:T(8,128)(2,1)}, bf16[1024,768]{1,0:T(8,128)(2,1)}) fusion(f32[1024]{0:T(1024)S(1)} %get-tuple-element.30, f32[1024,768]{1,0:T(8,128)S(1)} %fusion, f32[1024,768]{1,0:T(8,128)S(1)} %fusion.4, bf16[1024,2048]{1,0:T(8,128)(2,1)S(1)} %copy-done.1, ...), kind=kOutput, calls=%fused_computation.12 | convolution fusion | flops 3234594816 | bytes 18354176 | tf_op jit(solution)/shard_map/dot_general | solution.py:16
  131.7 26.5 %shard_map.110 = (bf16[1024,2048]{1,0:T(8,128)(2,1)}, bf16[1024,2048]{1,0:T(8,128)(2,1)}) custom-call(bf16[1024,768]{1,0:T(8,128)(2,1)} %get-tuple-element.19.refs_0_, bf16[1024,768]{1,0:T(8,128)(2,1)} %get-tuple-element.20.refs_1_, bf16[1024,768]{1,0:T(8,128)(2,1)} %get-tuple-element.21.refs_2_, bf16[1024,768]{1,0:T(8,128)(2,1)} %get-tuple-element.22.refs_3_, ...), custom_call_target="tpu_custom_call" | custom-call | flops 19327352832 | bytes 37748736 | tf_op jit(solution)/shard_map/pallas_call | solution.py:40
  158.2 0.0 reduce-scatter.3.cloned.1.call-update
  158.2 0.0 reduce-scatter.5.cloned.1.call-start
  158.3 0.5 reduce-scatter.5.cloned.1.call-update
  158.8 167.2 %shard_map.111 = bf16[6,512,768]{2,1,0:T(8,128)(2,1)} custom-call(bf16[1024,2048]{1,0:T(8,128)(2,1)} %all-gather.5.cloned.1.call-done.tok_hbm, bf16[1024,2048]{1,0:T(8,128)(2,1)} %all-gather.3.cloned.1.call-done.cot_hbm, bf16[1024,768]{1,0:T(8,128)(2,1)} %get-tuple-element.19.refs_0_, bf16[1024,768]{1,0:T(8,128)(2,1)} %get-tuple-element.20.refs_1_, ...), custom_call_target="tpu_custom_call" | custom-call | flops 154618822656 | bytes 25165824 | tf_op jit(solution)/shard_map/pallas_call | solution.py:158
  326.0 4.3 %slice_bitcast_fusion = (bf16[2,768,512]{1,2,0:T(8,128)(2,1)S(1)}, bf16[2,512,768]{2,1,0:T(8,128)(2,1)}, bf16[2,512,768]{2,1,0:T(8,128)(2,1)}) fusion(bf16[6,512,768]{2,1,0:T(8,128)(2,1)} %shard_map.111), kind=kLoop, calls=%fused_computation.28 | loop fusion | bytes 9437184 | tf_op jit(solution)/shard_map/transpose | solution.py:212
  330.4 1.6 copy.12
  331.9 0.0 reduce-scatter.3.cloned.1.call-done
  331.9 0.0 reduce-scatter.5.cloned.1.call-done
  (2 shorter events, 0.0 us)
Async XLA Ops:
  7.2 52.5 %all-gather.5.cloned.1.call-start = ((), (), s32[]{:S(2)}) async-start(), calls=%async_computation.3 | async-start | bytes 4718592 | tf_op jit(solution)/shard_map/all_gather | solution.py:187
  7.9 99.4 %all-gather.3.cloned.1.call-start = ((), (), s32[]{:S(2)}) async-start(), calls=%async_computation.2 | async-start | bytes 4718592 | tf_op jit(solution)/shard_map/all_gather | solution.py:188
  8.6 323.3 %reduce-scatter.3.cloned.1.call-start = ((), (), s32[]{:S(2)}) async-start(), calls=%async_computation.4 | async-start | bytes 4718592 | tf_op jit(solution)/shard_map/reduce_scatter | solution.py:225
  59.7 8.3 %copy-start = (bf16[1024,2048]{1,0:T(8,128)(2,1)S(1)}, bf16[1024,2048]{1,0:T(8,128)(2,1)}, u32[]{:S(2)}) copy-start(bf16[1024,2048]{1,0:T(8,128)(2,1)} %all-gather.5.cloned.1.call-done.tok_hbm) | copy-start | bytes 12582916
  107.3 6.4 %copy-start.2 = (bf16[1024,2048]{1,0:T(8,128)(2,1)S(1)}, bf16[1024,2048]{1,0:T(8,128)(2,1)}, u32[]{:S(2)}) copy-start(bf16[1024,2048]{1,0:T(8,128)(2,1)} %all-gather.3.cloned.1.call-done.cot_hbm) | copy-start | bytes 12582916
  107.3 11.9 %slice-start = ((s8[6291456]{0:T(1024)(128)(4,1)}), s8[4194304]{0:T(1024)(128)(4,1)S(1)}, s32[]{:S(2)}) async-start(s8[6291456]{0:T(1024)(128)(4,1)} %bitcast.30), calls=%async_computation.6 | async-start | bytes 8388608
  113.7 5.5 %slice-start.1 = ((s8[6291456]{0:T(1024)(128)(4,1)}), s8[2097152]{0:T(1024)(128)(4,1)S(1)}, s32[]{:S(2)}) async-start(s8[6291456]{0:T(1024)(128)(4,1)} %bitcast.30), calls=%async_computation.7 | async-start | bytes 4194304
  113.7 5.5 %copy-start.1 = (bf16[1024,2048]{1,0:T(8,128)(2,1)S(1)}, bf16[1024,2048]{1,0:T(8,128)(2,1)}, u32[]{:S(2)}) copy-start(bf16[1024,2048]{1,0:T(8,128)(2,1)} %all-gather.5.cloned.1.call-done.tok_hbm) | copy-start | bytes 12582916
  113.7 5.5 %copy-start.3 = (f32[1024,768]{1,0:T(8,128)S(1)}, f32[1024,768]{1,0:T(8,128)}, u32[]{:S(2)}) copy-start(f32[1024,768]{1,0:T(8,128)} %fusion.6) | copy-start | bytes 9437188
  158.2 173.7 %reduce-scatter.5.cloned.1.call-start = ((), (), s32[]{:S(2)}) async-start(), calls=%async_computation.5 | async-start | bytes 4718592 | tf_op jit(solution)/shard_map/reduce_scatter | solution.py:226
Sparse Core Ops, SparseCore 0:
  9.6 50.0 all-gather.4
  61.3 45.9 all-gather.2
  158.4 48.6 reduce-scatter.2
  209.8 48.1 reduce-scatter.4

commit v3 on v2

--- a/solution.py
+++ b/solution.py
@@ -16,51 +16,260 @@
     return lax.dot_general(a, b, (((ca,), (cb,)), ((), ())), preferred_element_type=F32)
 
 
-def outputs_kernel(homes, *refs):
-    gpg, gpu, hid = refs[:homes], refs[homes : 2 * homes], refs[2 * homes : 3 * homes]
-    gate, up, down, out, back = refs[3 * homes :]
-    acc = dot(hid[0][...], down[0], 1, 0)
+def gather_kernel(homes, tok, tile, tok_hbm, cot_hbm, mix_hbm, gate_hbm, up_hbm, down_hbm, *refs):
+    (xc_out, fac_out, xc, mix, gate, up, down, fac, in_sem, out_sem, line_recv, core_recv) = refs[:12]
+    up_send, down_send, core_send = refs[12:]
+    units = gate.shape[2]
+    tiles = units // tile
+    me = lax.axis_index("expert")
+    chips = lax.axis_size("expert") // 2
+    q, core = me // 2, me % 2
+    partner = me + 1 - 2 * core
+    first = me * homes
+
+    def rows_of(b, count):
+        return pl.ds(pl.multiple_of(b * tok, tok), count * tok)
+
+    own = [
+        pltpu.make_async_copy(tok_hbm, xc.at[0, rows_of(me, 1)], in_sem.at[0]),
+        pltpu.make_async_copy(cot_hbm, xc.at[1, rows_of(me, 1)], in_sem.at[1]),
+        pltpu.make_async_copy(mix_hbm, mix.at[me], in_sem.at[2]),
+    ]
+    weights = [
+        pltpu.make_async_copy(gate_hbm, gate, in_sem.at[3]),
+        pltpu.make_async_copy(up_hbm, up, in_sem.at[4]),
+        pltpu.make_async_copy(down_hbm, down, in_sem.at[5]),
+    ]
+    for load in own + weights:
+        load.start()
+
+    barrier = pltpu.get_barrier_semaphore()
+
+    def greet(peer):
+        pl.semaphore_signal(
+            barrier, inc=1, device_id={"expert": peer}, device_id_type=pl.DeviceIdType.MESH
+        )
+
+    greet(partner)
+
+    @pl.when(q > 0)
+    def _():
+        greet(me - 2)
+
+    @pl.when(q < chips - 1)
+    def _():
+        greet(me + 2)
+
+    pl.semaphore_wait(barrier, jnp.where((q > 0) & (q < chips - 1), 3, 2))
+    for load in own:
+        load.wait()
+
+    def moves(p, side, send, recv, peer):
+        b = 2 * p + side
+        return [
+            pltpu.make_async_remote_copy(
+                src_ref=ref,
+                dst_ref=ref,
+                send_sem=send.at[kind, p],
+                recv_sem=recv.at[kind, p],
+                device_id={"expert": peer},
+                device_id_type=pl.DeviceIdType.MESH,
+            )
+            for kind, ref in enumerate((mix.at[b], xc.at[:, rows_of(b, 1), :]))
+        ]
+
+    def go_up(p):
+        return moves(p, core, up_send, line_recv, me + 2)
+
+    def go_down(p):
+        return moves(p, core, down_send, line_recv, me - 2)
+
+    def go_core(p):
+        return moves(p, core, core_send, core_recv, partner)
+
+    def start(copies):
+        for copy in copies:
+            copy.start()
+
+    @pl.when(q < chips - 1)
+    def _():
+        start(go_up(q))
+
+    @pl.when(q > 0)
+    def _():
+        start(go_down(q))
+
+    start(go_core(q))
+    for load in weights:
+        load.wait()
+
+    def stored(p):
+        rows = rows_of(2 * p, 2)
+        return [
+            pltpu.make_async_copy(fac.at[:, rows, :], fac_out.at[:, rows, :], out_sem.at[0, p]),
+            pltpu.make_async_copy(xc.at[:, rows, :], xc_out.at[:, rows, :], out_sem.at[1, p]),
+        ]
+
+    def compute(p):
+        rows = rows_of(2 * p, 2)
+
+        @pl.loop(0, homes * tiles)
+        def _(i):
+            e = i // tiles
+            part = pl.ds(pl.multiple_of((i % tiles) * tile, tile), tile)
+            weight = jnp.concatenate(
+                [
+                    jnp.broadcast_to(mix[2 * p + side, first + e], (128, tok)).T[:, :1]
+                    for side in range(2)
+                ],
+                axis=0,
+            )
+            pre_gate = dot(xc[0, rows, :], gate[e, :, part], 1, 0)
+            pre_up = dot(xc[0, rows, :], up[e, :, part], 1, 0)
+            grad_hidden = dot(xc[1, rows, :], down[e, part, :], 1, 1) * weight
+            s = jax.nn.sigmoid(pre_gate)
+            act = pre_gate * s
+            gpg = grad_hidden * pre_up * s * (1.0 + pre_gate * (1.0 - s))
+            fac[e, rows, part] = gpg.astype(BF16)
+            fac[homes + e, rows, part] = (grad_hidden * act).astype(BF16)
+            fac[2 * homes + e, rows, part] = (weight * act * pre_up).astype(BF16)
+
+        start(stored(p))
+
+    @pl.loop(0, chips + 1)
+    def _(s):
+        below, above = q - s, q + s
+
+        @pl.when((s > 0) & (below >= 0))
+        def _():
+            for copy in moves(below, core, up_send, line_recv, me - 2):
+                copy.wait_recv()
+
+            @pl.when(q < chips - 1)
+            def _():
+                start(go_up(below))
+
+            start(go_core(below))
+
+        @pl.when((s > 0) & (above < chips))
+        def _():
+            for copy in moves(above, core, down_send, line_recv, me + 2):
+                copy.wait_recv()
+
+            @pl.when(q > 0)
+            def _():
+                start(go_down(above))
+
+            start(go_core(above))
+
+        @pl.loop(0, 2)
+        def _(side):
+            p = q + (2 * side - 1) * (s - 1)
+
+            @pl.when((s > side) & (p >= 0) & (p < chips))
+            def _():
+                for copy in moves(p, 1 - core, core_send, core_recv, partner):
+                    copy.wait_recv()
+                compute(p)
+
+    @pl.loop(0, chips)
+    def _(p):
+        for copy in stored(p):
+            copy.wait()
+        for copy in go_core(p):
+            copy.wait_send()
+
+        @pl.when((p <= q) & (q < chips - 1))
+        def _():
+            for copy in go_up(p):
+                copy.wait_send()
+
+        @pl.when((p >= q) & (q > 0))
+        def _():
+            for copy in go_down(p):
+                copy.wait_send()
+
+
+def gather_call(tokens, cotangent, mix, gate_matrix, up_matrix, down_matrix):
+    homes, width, units = gate_matrix.shape
+    tok = tokens.shape[0]
+    ways = lax.axis_size("expert")
+    rows, chips = tok * ways, ways // 2
+    dma = pltpu.SemaphoreType.DMA
+    hbm = pl.BlockSpec(memory_space=pl.ANY)
+    return pl.pallas_call(
+        functools.partial(gather_kernel, homes, tok, 256),
+        out_shape=[
+            jax.ShapeDtypeStruct((2, rows, width), BF16),
+            jax.ShapeDtypeStruct((3 * homes, rows, units), BF16),
+        ],
+        in_specs=[hbm] * 6,
+        out_specs=[hbm] * 2,
+        scratch_shapes=[
+            pltpu.VMEM((2, rows, width), BF16),
+            pltpu.VMEM((ways,) + mix.shape, F32),
+            pltpu.VMEM(gate_matrix.shape, BF16),
+            pltpu.VMEM(up_matrix.shape, BF16),
+            pltpu.VMEM(down_matrix.shape, BF16),
+            pltpu.VMEM((3 * homes, rows, units), BF16),
+            dma((6,)),
+            dma((2, chips)),
+            dma((2, chips)),
+            dma((2, chips)),
+            dma((2, chips)),
+            dma((2, chips)),
+            dma((2, chips)),
+        ],
+        compiler_params=pltpu.CompilerParams(
+            collective_id=1, has_side_effects=True, vmem_limit_bytes=56 * MIB
+        ),
+        cost_estimate=pl.CostEstimate(
+            flops=2 * rows * width * units * 3 * homes, bytes_accessed=40 * MIB, transcendentals=0
+        ),
+    )(tokens, cotangent, mix, gate_matrix, up_matrix, down_matrix)
+
+
+def outputs_kernel(homes, fac, gate, up, down, out, back):
+    acc = dot(fac[2 * homes], down[0], 1, 0)
     for e in range(1, homes):
-        acc += dot(hid[e][...], down[e], 1, 0)
+        acc += dot(fac[2 * homes + e], down[e], 1, 0)
     out[...] = acc.astype(BF16)
-    acc = dot(gpg[0][...], gate[0], 1, 1) + dot(gpu[0][...], up[0], 1, 1)
+    acc = dot(fac[0], gate[0], 1, 1) + dot(fac[homes], up[0], 1, 1)
     for e in range(1, homes):
-        acc += dot(gpg[e][...], gate[e], 1, 1) + dot(gpu[e][...], up[e], 1, 1)
+        acc += dot(fac[e], gate[e], 1, 1) + dot(fac[homes + e], up[e], 1, 1)
     back[...] = acc.astype(BF16)
 
 
 def outputs_call(factors, gate_matrix, up_matrix, down_matrix):
     homes, width, units = gate_matrix.shape
-    rows = factors[0].shape[0]
+    rows = factors.shape[1]
     tile = 256
-    whole = pl.BlockSpec((rows, units), lambda i: (0, 0))
     by_row = pl.BlockSpec((homes, tile, units), lambda i: (0, i, 0))
     by_col = pl.BlockSpec((homes, units, tile), lambda i: (0, 0, i))
-    flops = 2 * rows * units * width * 3 * homes
     return pl.pallas_call(
         functools.partial(outputs_kernel, homes),
         grid=(width // tile,),
         out_shape=[jax.ShapeDtypeStruct((rows, width), BF16)] * 2,
-        in_specs=[whole] * (3 * homes) + [by_row, by_row, by_col],
+        in_specs=[pl.BlockSpec(factors.shape, lambda i: (0, 0, 0)), by_row, by_row, by_col],
         out_specs=[pl.BlockSpec((rows, tile), lambda i: (0, i))] * 2,
         compiler_params=pltpu.CompilerParams(vmem_limit_bytes=56 * MIB),
-        cost_estimate=pl.CostEstimate(flops=flops, bytes_accessed=36 * MIB, transcendentals=0),
-    )(*factors, gate_matrix, up_matrix, down_matrix)
-
-
-def grads_kernel(count, cols, tok_hbm, cot_hbm, *refs):
-    factor_hbm = refs[:count]
-    (out, both, factor, turned, stage, relay, land, in_sem, send_sem, relay_sem, land_sem) = refs[count:]
+        cost_estimate=pl.CostEstimate(
+            flops=2 * rows * units * width * 3 * homes, bytes_accessed=36 * MIB, transcendentals=0
+        ),
+    )(factors, gate_matrix, up_matrix, down_matrix)
+
+
+def grads_kernel(count, cols, both_hbm, factor_hbm, *refs):
+    (out, both, factor, turned, stage, relay, land, in_sem, send_sem, relay_sem, land_sem) = refs
     split = 2 * count // 3
     me = lax.axis_index("dp")
     near_a = me + 1 - 2 * (me % 2)
     near_b = me + 2 - 4 * (me // 2)
     far = 3 - me
 
-    loads = [pltpu.make_async_copy(tok_hbm, both.at[0], in_sem.at[0])]
-    loads += [pltpu.make_async_copy(cot_hbm, both.at[1], in_sem.at[1])]
-    loads += [
-        pltpu.make_async_copy(factor_hbm[j], factor.at[j], in_sem.at[2 + j]) for j in range(count)
+    loads = [
+        pltpu.make_async_copy(both_hbm, both, in_sem.at[0]),
+        pltpu.make_async_copy(factor_hbm, factor, in_sem.at[1]),
     ]
     for load in loads:
         load.start()
@@ -148,17 +357,16 @@
         to_land(1, j, near_b).wait_send()
 
 
-def grads_call(all_tokens, all_cot, factors):
-    rows, width = all_tokens.shape
-    units = factors[0].shape[1]
-    count = len(factors)
+def grads_call(both, factors):
+    rows, width = both.shape[1:]
+    count, _, units = factors.shape
     cols = width // lax.axis_size("dp")
     piece = (cols, units)
     dma = pltpu.SemaphoreType.DMA
     return pl.pallas_call(
         functools.partial(grads_kernel, count, cols),
         out_shape=jax.ShapeDtypeStruct((count,) + piece, BF16),
-        in_specs=[pl.BlockSpec(memory_space=pl.ANY)] * (2 + count),
+        in_specs=[pl.BlockSpec(memory_space=pl.ANY)] * 2,
         out_specs=pl.BlockSpec(memory_space=pltpu.VMEM),
         scratch_shapes=[
             pltpu.VMEM((2, rows, width), BF16),
@@ -167,7 +375,7 @@
             pltpu.VMEM((3, count) + piece, BF16),
             pltpu.VMEM((count,) + piece, BF16),
             pltpu.VMEM((2, count) + piece, BF16),
-            dma((2 + count,)),
+            dma((2,)),
             dma((3, count)),
             dma((count,)),
             dma((2, count)),
@@ -178,18 +386,38 @@
         cost_estimate=pl.CostEstimate(
             flops=2 * rows * width * units * count * 8, bytes_accessed=24 * MIB, transcendentals=0
         ),
-    )(all_tokens, all_cot, *factors)
+    )(both, factors)
+
+
+def with_kernels(tokens, routes, route_gates, gate_matrix, up_matrix, down_matrix, cotangent):
+    homes = gate_matrix.shape[0]
+    experts = jnp.arange(homes * lax.axis_size("expert"), dtype=jnp.int32)
+    named = routes[None] == experts[:, None, None]
+    mix = jnp.sum(jnp.where(named, route_gates[None], 0.0), axis=2)[:, None, :]
+    both, factors = gather_call(tokens, cotangent, mix, gate_matrix, up_matrix, down_matrix)
+    out, back = outputs_call(factors, gate_matrix, up_matrix, down_matrix)
+    both, factors, out, back = lax.optimization_barrier((both, factors, out, back))
+    summed = grads_call(both, factors)
+    layer_out = lax.psum_scatter(out, "expert", scatter_dimension=0, tiled=True)
+    grad_tokens = lax.psum_scatter(back, "expert", scatter_dimension=0, tiled=True)
+    grad_gate, grad_up = summed[:homes], summed[homes : 2 * homes]
+    grad_down = jnp.swapaxes(summed[2 * homes :], 1, 2)
+    return (layer_out, grad_tokens, grad_gate, grad_up, grad_down)
 
 
 def per_device(tokens, routes, route_gates, gate_matrix, up_matrix, down_matrix, cotangent):
     homes, width, units = gate_matrix.shape
+    rows = tokens.shape[0] * lax.axis_size("expert")
+    fits = rows * (2 * width + 3 * homes * units) * 2 <= 18 * MIB
+    if fits and lax.axis_size("dp") == 4 and tokens.shape[0] == 128:
+        return with_kernels(
+            tokens, routes, route_gates, gate_matrix, up_matrix, down_matrix, cotangent
+        )
     first = lax.axis_index("expert") * homes
     all_tokens = lax.all_gather(tokens, "expert", axis=0, tiled=True)
     all_cot = lax.all_gather(cotangent, "expert", axis=0, tiled=True)
     all_routes = lax.all_gather(routes, "expert", axis=0, tiled=True)
     all_gates = lax.all_gather(route_gates, "expert", axis=0, tiled=True)
-    rows = all_tokens.shape[0]
-    kernels = rows * (2 * width + 3 * homes * units) * 2 <= 18 * MIB and lax.axis_size("dp") == 4
 
     hidden, gpgs, gpus = [], [], []
     for e in range(homes):
@@ -202,26 +430,17 @@
         hidden.append((weight * act * pre_up).astype(BF16))
         gpgs.append((grad_hidden * pre_up * s * (1.0 + pre_gate * (1.0 - s))).astype(BF16))
         gpus.append((grad_hidden * act).astype(BF16))
-
-    if kernels:
-        factors = gpgs + gpus + hidden
-        out, back = outputs_call(factors, gate_matrix, up_matrix, down_matrix)
-        factors, out, back = lax.optimization_barrier((factors, out, back))
-        summed = grads_call(all_tokens, all_cot, factors)
-        grad_gate, grad_up = summed[:homes], summed[homes : 2 * homes]
-        grad_down = jnp.swapaxes(summed[2 * homes :], 1, 2)
-    else:
-        part_gate = jnp.stack([dot(all_tokens, g, 0, 0).astype(BF16) for g in gpgs])
-        part_up = jnp.stack([dot(all_tokens, g, 0, 0).astype(BF16) for g in gpus])
-        part_down = jnp.stack([dot(h, all_cot, 0, 0).astype(BF16) for h in hidden])
-        grad_gate = lax.psum_scatter(part_gate, "dp", scatter_dimension=1, tiled=True)
-        grad_up = lax.psum_scatter(part_up, "dp", scatter_dimension=1, tiled=True)
-        grad_down = lax.psum_scatter(part_down, "dp", scatter_dimension=2, tiled=True)
-        out = sum(dot(h, down_matrix[e], 1, 0) for e, h in enumerate(hidden)).astype(BF16)
-        back = sum(
-            dot(gpgs[e], gate_matrix[e], 1, 1) + dot(gpus[e], up_matrix[e], 1, 1)
-            for e in range(homes)
-        ).astype(BF16)
+    part_gate = jnp.stack([dot(all_tokens, g, 0, 0).astype(BF16) for g in gpgs])
+    part_up = jnp.stack([dot(all_tokens, g, 0, 0).astype(BF16) for g in gpus])
+    part_down = jnp.stack([dot(h, all_cot, 0, 0).astype(BF16) for h in hidden])
+    grad_gate = lax.psum_scatter(part_gate, "dp", scatter_dimension=1, tiled=True)
+    grad_up = lax.psum_scatter(part_up, "dp", scatter_dimension=1, tiled=True)
+    grad_down = lax.psum_scatter(part_down, "dp", scatter_dimension=2, tiled=True)
+    out = sum(dot(h, down_matrix[e], 1, 0) for e, h in enumerate(hidden)).astype(BF16)
+    back = sum(
+        dot(gpgs[e], gate_matrix[e], 1, 1) + dot(gpus[e], up_matrix[e], 1, 1)
+        for e in range(homes)
+    ).astype(BF16)
     layer_out = lax.psum_scatter(out, "expert", scatter_dimension=0, tiled=True)
     grad_tokens = lax.psum_scatter(back, "expert", scatter_dimension=0, tiled=True)
     return (layer_out, grad_tokens, grad_gate, grad_up, grad_down)

time: 339 us -> 304 us (0.90)
  Pallas kernels: 194 us -> 282 us
  waiting for transfers between devices: 56.5 us -> 0.53 us
  matrix products: 38.2 us -> 0 us
  blocking collectives: 30.1 us -> 0 us
    pallas_call x0 -> x1, Pallas kernels: none -> 90.7 us  [gather_call(): pl.pallas_call(functools.partial(gather_kernel, homes, tok, 256), out_sha...]
    all_gather x2 -> x0, waiting for transfers between devices: 54.6 us -> none  [the longest x1 33.7 us: per_device(): all_cot = lax.all_gather(cotangent, 'expert', axis=0, tiled=True)]
    dot_general x6 -> x0, matrix products: 38.2 us -> none  [dot(): lax.dot_general(a, b, (((ca,), (cb,)), ((), ())), preferred_element_type=...]
    all_gather x2 -> x0, blocking collectives: 30.1 us -> none  [the longest x1 15.8 us: per_device(): all_gates = lax.all_gather(route_gates, 'expert', axis=0, tiled=True)]
  transfers between devices with their start and end apart: 4 -> 2, of which waited for: 2 -> 0; matrix products, arithmetic and copies ran while one was open for 6% -> 2% of each run, Pallas kernels for 49% -> 54%
where the time goes in v3:
time: 304 us
  Pallas kernels  282 us (93%)
  between operations  14.1 us (5%)
  local copies, waits for them, and re-layouts  5.89 us (2%)
    pallas_call x1, Pallas kernels, grads_call(): pl.pallas_call(functools.partial(grads_kernel, count, cols), out_shape=ja...  164 us
    pallas_call x1, Pallas kernels, gather_call(): pl.pallas_call(functools.partial(gather_kernel, homes, tok, 256), out_sha...  90.7 us
    pallas_call x1, Pallas kernels, outputs_call(): pl.pallas_call(functools.partial(outputs_kernel, homes), grid=(width // t...  26.4 us
  transfers between devices with their start and end apart: 2, of which 0 were waited for; matrix products, arithmetic and copies ran while one was open for 2% of the time, Pallas kernels for 54%

profile of v3, /device:TPU:0, one launch (start us, length us, event | category | flops | bytes accessed | tf_op | source)
XLA Modules:
  0.0 303.6 jit_solution(9118473179033074565)
XLA Ops:
  7.2 0.0 reduce-scatter.3.cloned.1.call-start
  7.2 1.3 select_reduce_fusion
  8.5 90.7 %shard_map.110 = (bf16[2,1024,2048]{2,1,0:T(8,128)(2,1)}, bf16[6,1024,768]{2,1,0:T(8,128)(2,1)}) custom-call(bf16[128,2048]{1,0:T(8,128)(2,1)} %tok_hbm.1, bf16[128,2048]{1,0:T(8,128)(2,1)} %cot_hbm.1, f32[16,1,128]{2,1,0:T(1,128)} %bitcast.3, bf16[2,2048,768]{2,1,0:T(8,128)(2,1)} %gate.1, bf16[2,2048,768]{2,1,0:T(8,128)(2,1)} %up.1, bf16[2,768,2048]{2,1,0:T(8,128)(2,1)} %down.1), custom_call_target="tpu_custom_call" | custom-call | flops 19327352832 | bytes 41943040 | tf_op jit(solution)/shard_map/pallas_call | solution.py:200
  99.3 26.4 %shard_map.111 = (bf16[1024,2048]{1,0:T(8,128)(2,1)}, bf16[1024,2048]{1,0:T(8,128)(2,1)}) custom-call(bf16[6,1024,768]{2,1,0:T(8,128)(2,1)} %get-tuple-element.20.fac.factor_hbm, bf16[2,2048,768]{2,1,0:T(8,128)(2,1)} %gate.1, bf16[2,2048,768]{2,1,0:T(8,128)(2,1)} %up.1, bf16[2,768,2048]{2,1,0:T(8,128)(2,1)} %down.1), custom_call_target="tpu_custom_call" | custom-call | flops 19327352832 | bytes 37748736 | tf_op jit(solution)/shard_map/pallas_call | solution.py:249
  125.7 0.0 reduce-scatter.3.cloned.1.call-update
  125.7 0.2 reduce-scatter.5.cloned.1.call-start
  125.9 0.5 reduce-scatter.5.cloned.1.call-update
  126.5 164.4 %shard_map.112 = bf16[6,512,768]{2,1,0:T(8,128)(2,1)} custom-call(bf16[2,1024,2048]{2,1,0:T(8,128)(2,1)} %get-tuple-element.19.both_hbm, bf16[6,1024,768]{2,1,0:T(8,128)(2,1)} %get-tuple-element.20.fac.factor_hbm), custom_call_target="tpu_custom_call" | custom-call | flops 154618822656 | bytes 25165824 | tf_op jit(solution)/shard_map/pallas_call | solution.py:366
  290.9 4.3 %slice_bitcast_fusion = (bf16[2,768,512]{1,2,0:T(8,128)(2,1)S(1)}, bf16[2,512,768]{2,1,0:T(8,128)(2,1)}, bf16[2,512,768]{2,1,0:T(8,128)(2,1)}) fusion(bf16[6,512,768]{2,1,0:T(8,128)(2,1)} %shard_map.112), kind=kLoop, calls=%fused_computation | loop fusion | bytes 9437184 | tf_op jit(solution)/shard_map/transpose | solution.py:404
  295.2 1.6 copy.15
  296.8 0.0 reduce-scatter.3.cloned.1.call-done
  296.8 0.0 reduce-scatter.5.cloned.1.call-done
Async XLA Ops:
  7.2 289.6 %reduce-scatter.3.cloned.1.call-start = ((), (), s32[]{:S(2)}) async-start(), calls=%async_computation.2 | async-start | bytes 4718592 | tf_op jit(solution)/shard_map/reduce_scatter | solution.py:401
  125.7 171.1 %reduce-scatter.5.cloned.1.call-start = ((), (), s32[]{:S(2)}) async-start(), calls=%async_computation.3 | async-start | bytes 4718592 | tf_op jit(solution)/shard_map/reduce_scatter | solution.py:402
Sparse Core Ops, SparseCore 0:
  125.8 48.2 reduce-scatter.2
  177.0 48.1 reduce-scatter.4

commit v4 on v3

--- a/solution.py
+++ b/solution.py
@@ -17,8 +17,8 @@
 
 
 def gather_kernel(homes, tok, tile, tok_hbm, cot_hbm, mix_hbm, gate_hbm, up_hbm, down_hbm, *refs):
-    (xc_out, fac_out, xc, mix, gate, up, down, fac, in_sem, out_sem, line_recv, core_recv) = refs[:12]
-    up_send, down_send, core_send = refs[12:]
+    (xc_out, fac_out, sum_out, sum_back, xc, mix, gate, up, down, fac, sums) = refs[:11]
+    in_sem, out_sem, line_recv, core_recv, up_send, down_send, core_send = refs[11:]
     units = gate.shape[2]
     tiles = units // tile
     me = lax.axis_index("expert")
@@ -108,6 +108,8 @@
         return [
             pltpu.make_async_copy(fac.at[:, rows, :], fac_out.at[:, rows, :], out_sem.at[0, p]),
             pltpu.make_async_copy(xc.at[:, rows, :], xc_out.at[:, rows, :], out_sem.at[1, p]),
+            pltpu.make_async_copy(sums.at[0, rows, :], sum_out.at[rows, :], out_sem.at[2, p]),
+            pltpu.make_async_copy(sums.at[1, rows, :], sum_back.at[rows, :], out_sem.at[3, p]),
         ]
 
     def compute(p):
@@ -134,9 +136,22 @@
             fac[homes + e, rows, part] = (grad_hidden * act).astype(BF16)
             fac[2 * homes + e, rows, part] = (weight * act * pre_up).astype(BF16)
 
+        @pl.loop(0, gate.shape[1] // tile)
+        def _(i):
+            part = pl.ds(pl.multiple_of(i * tile, tile), tile)
+            out = dot(fac[2 * homes, rows, :], down[0, :, part], 1, 0)
+            back = dot(fac[0, rows, :], gate[0, part, :], 1, 1)
+            back += dot(fac[homes, rows, :], up[0, part, :], 1, 1)
+            for e in range(1, homes):
+                out += dot(fac[2 * homes + e, rows, :], down[e, :, part], 1, 0)
+                back += dot(fac[e, rows, :], gate[e, part, :], 1, 1)
+                back += dot(fac[homes + e, rows, :], up[e, part, :], 1, 1)
+            sums[0, rows, part] = out.astype(BF16)
+            sums[1, rows, part] = back.astype(BF16)
+
         start(stored(p))
 
-    @pl.loop(0, chips + 1)
+    @pl.loop(0, chips)
     def _(s):
         below, above = q - s, q + s
 
@@ -164,9 +179,9 @@
 
         @pl.loop(0, 2)
         def _(side):
-            p = q + (2 * side - 1) * (s - 1)
-
-            @pl.when((s > side) & (p >= 0) & (p < chips))
+            p = q + (2 * side - 1) * s
+
+            @pl.when((s >= side) & (p >= 0) & (p < chips))
             def _():
                 for copy in moves(p, 1 - core, core_send, core_recv, partner):
                     copy.wait_recv()
@@ -202,9 +217,11 @@
         out_shape=[
             jax.ShapeDtypeStruct((2, rows, width), BF16),
             jax.ShapeDtypeStruct((3 * homes, rows, units), BF16),
+            jax.ShapeDtypeStruct((rows, width), BF16),
+            jax.ShapeDtypeStruct((rows, width), BF16),
         ],
         in_specs=[hbm] * 6,
-        out_specs=[hbm] * 2,
+        out_specs=[hbm] * 4,
         scratch_shapes=[
             pltpu.VMEM((2, rows, width), BF16),
             pltpu.VMEM((ways,) + mix.shape, F32),
@@ -212,8 +229,9 @@
             pltpu.VMEM(up_matrix.shape, BF16),
             pltpu.VMEM(down_matrix.shape, BF16),
             pltpu.VMEM((3 * homes, rows, units), BF16),
+            pltpu.VMEM((2, rows, width), BF16),
             dma((6,)),
-            dma((2, chips)),
+            dma((4, chips)),
             dma((2, chips)),
             dma((2, chips)),
             dma((2, chips)),
@@ -221,42 +239,12 @@
             dma((2, chips)),
         ],
         compiler_params=pltpu.CompilerParams(
-            collective_id=1, has_side_effects=True, vmem_limit_bytes=56 * MIB
+            collective_id=1, has_side_effects=True, vmem_limit_bytes=60 * MIB
         ),
         cost_estimate=pl.CostEstimate(
-            flops=2 * rows * width * units * 3 * homes, bytes_accessed=40 * MIB, transcendentals=0
+            flops=2 * rows * width * units * 6 * homes, bytes_accessed=56 * MIB, transcendentals=0
         ),
     )(tokens, cotangent, mix, gate_matrix, up_matrix, down_matrix)
-
-
-def outputs_kernel(homes, fac, gate, up, down, out, back):
-    acc = dot(fac[2 * homes], down[0], 1, 0)
-    for e in range(1, homes):
-        acc += dot(fac[2 * homes + e], down[e], 1, 0)
-    out[...] = acc.astype(BF16)
-    acc = dot(fac[0], gate[0], 1, 1) + dot(fac[homes], up[0], 1, 1)
-    for e in range(1, homes):
-        acc += dot(fac[e], gate[e], 1, 1) + dot(fac[homes + e], up[e], 1, 1)
-    back[...] = acc.astype(BF16)
-
-
-def outputs_call(factors, gate_matrix, up_matrix, down_matrix):
-    homes, width, units = gate_matrix.shape
-    rows = factors.shape[1]
-    tile = 256
-    by_row = pl.BlockSpec((homes, tile, units), lambda i: (0, i, 0))
-    by_col = pl.BlockSpec((homes, units, tile), lambda i: (0, 0, i))
-    return pl.pallas_call(
-        functools.partial(outputs_kernel, homes),
-        grid=(width // tile,),
-        out_shape=[jax.ShapeDtypeStruct((rows, width), BF16)] * 2,
-        in_specs=[pl.BlockSpec(factors.shape, lambda i: (0, 0, 0)), by_row, by_row, by_col],
-        out_specs=[pl.BlockSpec((rows, tile), lambda i: (0, i))] * 2,
-        compiler_params=pltpu.CompilerParams(vmem_limit_bytes=56 * MIB),
-        cost_estimate=pl.CostEstimate(
-            flops=2 * rows * units * width * 3 * homes, bytes_accessed=36 * MIB, transcendentals=0
-        ),
-    )(factors, gate_matrix, up_matrix, down_matrix)
 
 
 def grads_kernel(count, cols, both_hbm, factor_hbm, *refs):
@@ -394,8 +382,9 @@
     experts = jnp.arange(homes * lax.axis_size("expert"), dtype=jnp.int32)
     named = routes[None] == experts[:, None, None]
     mix = jnp.sum(jnp.where(named, route_gates[None], 0.0), axis=2)[:, None, :]
-    both, factors = gather_call(tokens, cotangent, mix, gate_matrix, up_matrix, down_matrix)
-    out, back = outputs_call(factors, gate_matrix, up_matrix, down_matrix)
+    both, factors, out, back = gather_call(
+        tokens, cotangent, mix, gate_matrix, up_matrix, down_matrix
+    )
     both, factors, out, back = lax.optimization_barrier((both, factors, out, back))
     summed = grads_call(both, factors)
     layer_out = lax.psum_scatter(out, "expert", scatter_dimension=0, tiled=True)

time: 304 us -> 285 us (0.938)
  Pallas kernels: 282 us -> 263 us
    pallas_call x1 -> x0, Pallas kernels: 26.4 us -> none  [outputs_call(): pl.pallas_call(functools.partial(outputs_kernel, homes), grid=(width // t...]
    pallas_call x1, Pallas kernels: 90.7 us -> 96.6 us  [gather_call(): pl.pallas_call(functools.partial(gather_kernel, homes, tok, 256), out_sha...]
  transfers between devices with their start and end apart: 2 -> 2, of which waited for: 0 -> 0; matrix products, arithmetic and copies ran while one was open for 2% -> 2% of each run, Pallas kernels for 54% -> 58%
where the time goes in v4:
time: 285 us
  Pallas kernels  263 us (92%)
  between operations  14.1 us (5%)
  local copies, waits for them, and re-layouts  5.89 us (2%)
    pallas_call x1, Pallas kernels, grads_call(): pl.pallas_call(functools.partial(grads_kernel, count, cols), out_shape=ja...  166 us
    pallas_call x1, Pallas kernels, gather_call(): pl.pallas_call(functools.partial(gather_kernel, homes, tok, 256), out_sha...  96.6 us
  transfers between devices with their start and end apart: 2, of which 0 were waited for; matrix products, arithmetic and copies ran while one was open for 2% of the time, Pallas kernels for 58%

profile of v4, /device:TPU:0, one launch (start us, length us, event | category | flops | bytes accessed | tf_op | source)
XLA Modules:
  0.0 284.9 jit_solution(4686788145357005907)
XLA Ops:
  7.2 0.0 reduce-scatter.3.cloned.1.call-start
  7.2 1.3 select_reduce_fusion
  8.5 96.6 %shard_map.110 = (bf16[2,1024,2048]{2,1,0:T(8,128)(2,1)}, bf16[6,1024,768]{2,1,0:T(8,128)(2,1)}, bf16[1024,2048]{1,0:T(8,128)(2,1)}, bf16[1024,2048]{1,0:T(8,128)(2,1)}) custom-call(bf16[128,2048]{1,0:T(8,128)(2,1)} %tok_hbm.1, bf16[128,2048]{1,0:T(8,128)(2,1)} %cot_hbm.1, f32[16,1,128]{2,1,0:T(1,128)} %bitcast.3, bf16[2,2048,768]{2,1,0:T(8,128)(2,1)} %gate_hbm.1, ...), custom_call_target="tpu_custom_call" | custom-call | flops 38654705664 | bytes 58720256 | tf_op jit(solution)/shard_map/pallas_call | solution.py:215
  105.2 0.0 reduce-scatter.3.cloned.1.call-update
  105.2 0.0 reduce-scatter.5.cloned.1.call-start
  105.2 0.7 reduce-scatter.5.cloned.1.call-update
  105.9 166.2 %shard_map.111 = bf16[6,512,768]{2,1,0:T(8,128)(2,1)} custom-call(bf16[2,1024,2048]{2,1,0:T(8,128)(2,1)} %get-tuple-element.11.both_hbm, bf16[6,1024,768]{2,1,0:T(8,128)(2,1)} %get-tuple-element.12.factor_hbm), custom_call_target="tpu_custom_call" | custom-call | flops 154618822656 | bytes 25165824 | tf_op jit(solution)/shard_map/pallas_call | solution.py:354
  272.2 4.3 %slice_bitcast_fusion = (bf16[2,768,512]{1,2,0:T(8,128)(2,1)S(1)}, bf16[2,512,768]{2,1,0:T(8,128)(2,1)}, bf16[2,512,768]{2,1,0:T(8,128)(2,1)}) fusion(bf16[6,512,768]{2,1,0:T(8,128)(2,1)} %shard_map.111), kind=kLoop, calls=%fused_computation | loop fusion | bytes 9437184 | tf_op jit(solution)/shard_map/transpose | solution.py:393
  276.5 1.6 copy.15
  278.1 0.0 reduce-scatter.3.cloned.1.call-done
  278.1 0.0 reduce-scatter.5.cloned.1.call-done
Async XLA Ops:
  7.2 270.9 %reduce-scatter.3.cloned.1.call-start = ((), (), s32[]{:S(2)}) async-start(), calls=%async_computation.2 | async-start | bytes 4718592 | tf_op jit(solution)/shard_map/reduce_scatter | solution.py:390
  105.2 172.9 %reduce-scatter.5.cloned.1.call-start = ((), (), s32[]{:S(2)}) async-start(), calls=%async_computation.3 | async-start | bytes 4718592 | tf_op jit(solution)/shard_map/reduce_scatter | solution.py:391
Sparse Core Ops, SparseCore 0:
  105.3 50.1 reduce-scatter.2
  158.4 48.1 reduce-scatter.4
